TPU v7x, 512 devices: a whole 4x8x8 slice. The times are simulated.
512 devices in a mesh: sec: 8 (over y_hi, x), space: 64 (over z, y_lo, core).
Axes of the slice: x: 4, y: 8 (y_hi: 2, y_lo: 4; y = y_hi * 4 + y_lo), z: 8, core: 2. Of those that a mesh axis runs over, the one named last changes fastest.
Arguments:
- density: float32 [64, 256, 64, 128], P('sec', 'space'), may hold values from 0.1 to 2
- wind_speed: float32 [256, 64, 128], P('space'), may hold values from -0.35 to 0.35
- settling: float32 [64], P('sec'), may hold values from 0.05 to 0.25
- diffusion: float32 [64], P('sec'), may hold values from 0.01 to 0.06
- breakup: bfloat16 [64, 64], replicated, may hold values from -0.375 to 0.375
- coag_kernel: float32 [64, 64], replicated, may hold values from 0.0025 to 0.02
- pair_target: int32 [64, 64], replicated, may hold values from 0 to 63, as said below
Outputs:
- updated: float32 [64, 256, 64, 128], P('sec', 'space')
Inputs may be any that keep to these rules, and one draw needn't show every extreme that they name: pair_target[i,j] is at least the larger of i and j.
All inputs are finite; a program needn't handle non-finite values.
Results may differ from a plain program's by a relative error of at most 0.0012.
Values may be sent and summed in bfloat16 or wider, within the bound.
No kernel may reach another device: no remote copies, remote signals or barrier semaphores. Data moves between devices by JAX's collectives and lax.ppermute only.
A program may use at most 64 MiB of HBM per device.

v0:
```python
import jax
import jax.numpy as jnp
from jax import lax
from jax.sharding import PartitionSpec as P

SUBSTEPS = 2


def with_halo(block, sides, width):
    for axis, dim in sides:
        count = lax.axis_size(axis)
        forward = [(i, i + 1) for i in range(count - 1)]
        backward = [(target, source) for source, target in forward]
        low = lax.ppermute(
            lax.slice_in_dim(block, block.shape[dim] - width, None, axis=dim), axis, forward
        )
        high = lax.ppermute(lax.slice_in_dim(block, 0, width, axis=dim), axis, backward)
        block = jnp.concatenate([low, block, high], axis=dim)
    return block


def advect(padded, wind_speed, settling, diffusion):
    center = padded[:, 1:-1]
    west_cell = padded[:, :-2]
    east_cell = padded[:, 2:]
    spread = jnp.pad(center, ((0, 0), (0, 0), (1, 1), (1, 1)))
    north_cell = spread[:, :, 2:, 1:-1]
    south_cell = spread[:, :, :-2, 1:-1]
    above_cell = spread[:, :, 1:-1, 2:]
    below_cell = spread[:, :, 1:-1, :-2]
    forward = jnp.maximum(wind_speed, 0.0)
    backward = jnp.minimum(wind_speed, 0.0)
    advected = forward * (center - west_cell) + backward * (east_cell - center)
    settled = settling[:, None, None, None] * (above_cell - center)
    laplace = (
        west_cell + east_cell + north_cell + south_cell + above_cell + below_cell - 6.0 * center
    )
    return center - advected + settled + diffusion[:, None, None, None] * laplace


def kinetics(cells_block, breakup, kernel_bf, pair_table):
    sections = cells_block.shape[0]
    fragments = jnp.dot(breakup, cells_block, preferred_element_type=jnp.float32)
    loss_rate = jnp.dot(kernel_bf, cells_block, preferred_element_type=jnp.float32)
    pair_sums = jnp.dot(pair_table, cells_block, preferred_element_type=jnp.float32)
    pair_sums = pair_sums.reshape(sections, sections, -1)
    as_float = cells_block.astype(jnp.float32)
    gained = jnp.sum(as_float[:, None, :] * pair_sums, axis=0)
    return (fragments + gained - as_float * loss_rate).astype(jnp.bfloat16)


def per_device(density, wind_speed, settling, diffusion, breakup, coag_kernel, pair_target):
    field = density
    for step_index in range(SUBSTEPS):
        padded = with_halo(field, (("space", 1),), 1)
        field = advect(padded, wind_speed, settling, diffusion)
    sec_local = field.shape[0]
    rounded = field.astype(jnp.bfloat16).reshape(sec_local, -1)
    gathered = lax.all_to_all(rounded, "sec", split_axis=1, concat_axis=0, tiled=True)
    sections = gathered.shape[0]
    targets = jnp.arange(sections, dtype=jnp.int32)
    onehot = (pair_target[:, :, None] == targets[None, None, :]).astype(jnp.float32)
    pair_table = (
        jnp.transpose(coag_kernel[:, :, None] * onehot, (0, 2, 1))
        .reshape(sections * sections, sections)
        .astype(jnp.bfloat16)
    )
    kernel_bf = coag_kernel.astype(jnp.bfloat16)
    local_cells = gathered.shape[1]
    block_size = 512
    blocks = jnp.transpose(
        gathered.reshape(sections, local_cells // block_size, block_size), (1, 0, 2)
    )
    tendency = lax.map(
        lambda cells_block: kinetics(cells_block, breakup, kernel_bf, pair_table), blocks
    )
    tendency = jnp.transpose(tendency, (1, 0, 2)).reshape(sections, local_cells)
    returned = lax.all_to_all(tendency, "sec", split_axis=0, concat_axis=1, tiled=True)
    return field + 0.25 * returned.reshape(field.shape).astype(jnp.float32)


def solution(mesh):
    in_specs = (
        P("sec", "space", None, None),
        P("space", None, None),
        P("sec"),
        P("sec"),
        P(),
        P(),
        P(),
    )
    out_specs = P("sec", "space", None, None)
    return jax.shard_map(
        per_device, mesh=mesh, in_specs=in_specs, out_specs=out_specs, check_vma=False
    )
```

profile of v0, /device:TPU:336, one launch (start us, length us, event | category | flops | bytes accessed | tf_op | source)
XLA Modules:
  0.0 237.6 jit_solution(12535437537774180883)
XLA Ops:
  11.3 5.1 %fusion.24 = f32[8,4,64,128]{3,2,1,0:T(8,128)S(1)} fusion(f32[8,4,64,128]{3,2,1,0:T(8,128)} %param.9, f32[8,1,64,128]{3,2,1,0:T(8,128)S(1)} %collective-permute-done.1, f32[8,1,64,128]{3,2,1,0:T(8,128)S(1)} %collective-permute-done, f32[8]{0:T(128)} %param.12, f32[8]{0:T(128)} %param.11, f32[4,64,128]{2,1,0:T(8,128)S(1)} %get-tuple-element.98, ...), kind=kLoop, calls=%fused_computation.38 | loop fusion | flops 5242880 | bytes 2883648 | tf_op jit(solution)/shard_map/add | solution.py:38
  31.8 9.7 %all-to-all-start = ((bf16[8,8,4096]{2,0,1:T(8,128)(2,1)}), bf16[8,8,4096]{2,0,1:T(8,128)(2,1)S(1)}, u32[]{:S(2)}, u32[]{:S(2)}) async-start(bf16[8,8,4096]{2,0,1:T(8,128)(2,1)} %copy.14), calls=%async_computation | async-start | bytes 1048576 | tf_op jit(solution)/shard_map/all_to_all | solution.py:59
  41.6 19.4 %all-to-all-done = bf16[8,8,4096]{2,0,1:T(8,128)(2,1)S(1)} async-done(((bf16[8,8,4096]{2,0,1:T(8,128)(2,1)}), bf16[8,8,4096]{2,0,1:T(8,128)(2,1)S(1)}, u32[]{:S(2)}, u32[]{:S(2)}) %all-to-all-start) | async-done | bytes 524320 | tf_op jit(solution)/shard_map/all_to_all | solution.py:59
  61.4 154.1 %while.11 = (s32[]{:T(128)}, bf16[8,64,512]{2,1,0:T(8,128)(2,1)S(1)}, bf16[8,64,512]{2,1,0:T(8,128)(2,1)S(1)}, bf16[64,64]{1,0:T(8,128)(2,1)S(1)}, bf16[64,64]{1...) while((s32[]{:T(128)}, ...), condition=%wide.region_2.3_spmd.clone, body=%wide.region_0.2_spmd.clone.sunk | while | flops 281706496 | bytes 36382820 | solution.py:74
  66.6 9.0 %copy.20 = f32[4096,512]{1,0:T(8,128)} copy(f32[4096,512]{0,1:T(8,128)} %convolution_bitcast_fusion.4) | data formatting | bytes 16777216 | tf_op jit(solution)/shard_map/while/body/eval_jaxpr/dot_general | solution.py:45
  75.6 4.7 %multiply_reduce_fusion.2 = f32[64,512]{1,0:T(8,128)S(1)} fusion(f32[64,64,512]{2,1,0:T(8,128)} %bitcast.85, f32[64,512]{1,0:T(8,128)S(1)} %bitcast_convert_fusion.2), kind=kLoop, calls=%fused_computation.1.clone.1 | loop fusion | flops 4161536 | bytes 8650752 | tf_op jit(solution)/shard_map/while/body/eval_jaxpr/reduce_sum | solution.py:48
  81.4 4.5 %convolution_bitcast_fusion.4 = f32[4096,512]{0,1:T(8,128)} fusion(bf16[4096,64]{1,0:T(8,128)(2,1)S(1)} %fusion.72, bf16[8,64,512]{2,1,0:T(8,128)(2,1)S(1)} %get-tuple-element.170, s32[]{:T(128)} %get-tuple-element.159), kind=kOutput, calls=%fused_computation.2.clone.1 | convolution fusion | flops 268435456 | bytes 9502724 | tf_op jit(solution)/shard_map/while/body/eval_jaxpr/dot_general | solution.py:45
  85.9 9.0 %copy.20 = f32[4096,512]{1,0:T(8,128)} copy(f32[4096,512]{0,1:T(8,128)} %convolution_bitcast_fusion.4) | data formatting | bytes 16777216 | tf_op jit(solution)/shard_map/while/body/eval_jaxpr/dot_general | solution.py:45
  94.9 4.7 %multiply_reduce_fusion.2 = f32[64,512]{1,0:T(8,128)S(1)} fusion(f32[64,64,512]{2,1,0:T(8,128)} %bitcast.85, f32[64,512]{1,0:T(8,128)S(1)} %bitcast_convert_fusion.2), kind=kLoop, calls=%fused_computation.1.clone.1 | loop fusion | flops 4161536 | bytes 8650752 | tf_op jit(solution)/shard_map/while/body/eval_jaxpr/reduce_sum | solution.py:48
  100.6 4.5 %convolution_bitcast_fusion.4 = f32[4096,512]{0,1:T(8,128)} fusion(bf16[4096,64]{1,0:T(8,128)(2,1)S(1)} %fusion.72, bf16[8,64,512]{2,1,0:T(8,128)(2,1)S(1)} %get-tuple-element.170, s32[]{:T(128)} %get-tuple-element.159), kind=kOutput, calls=%fused_computation.2.clone.1 | convolution fusion | flops 268435456 | bytes 9502724 | tf_op jit(solution)/shard_map/while/body/eval_jaxpr/dot_general | solution.py:45
  105.2 9.0 %copy.20 = f32[4096,512]{1,0:T(8,128)} copy(f32[4096,512]{0,1:T(8,128)} %convolution_bitcast_fusion.4) | data formatting | bytes 16777216 | tf_op jit(solution)/shard_map/while/body/eval_jaxpr/dot_general | solution.py:45
  114.2 4.7 %multiply_reduce_fusion.2 = f32[64,512]{1,0:T(8,128)S(1)} fusion(f32[64,64,512]{2,1,0:T(8,128)} %bitcast.85, f32[64,512]{1,0:T(8,128)S(1)} %bitcast_convert_fusion.2), kind=kLoop, calls=%fused_computation.1.clone.1 | loop fusion | flops 4161536 | bytes 8650752 | tf_op jit(solution)/shard_map/while/body/eval_jaxpr/reduce_sum | solution.py:48
  119.9 4.5 %convolution_bitcast_fusion.4 = f32[4096,512]{0,1:T(8,128)} fusion(bf16[4096,64]{1,0:T(8,128)(2,1)S(1)} %fusion.72, bf16[8,64,512]{2,1,0:T(8,128)(2,1)S(1)} %get-tuple-element.170, s32[]{:T(128)} %get-tuple-element.159), kind=kOutput, calls=%fused_computation.2.clone.1 | convolution fusion | flops 268435456 | bytes 9502724 | tf_op jit(solution)/shard_map/while/body/eval_jaxpr/dot_general | solution.py:45
  124.4 9.0 %copy.20 = f32[4096,512]{1,0:T(8,128)} copy(f32[4096,512]{0,1:T(8,128)} %convolution_bitcast_fusion.4) | data formatting | bytes 16777216 | tf_op jit(solution)/shard_map/while/body/eval_jaxpr/dot_general | solution.py:45
  133.4 4.7 %multiply_reduce_fusion.2 = f32[64,512]{1,0:T(8,128)S(1)} fusion(f32[64,64,512]{2,1,0:T(8,128)} %bitcast.85, f32[64,512]{1,0:T(8,128)S(1)} %bitcast_convert_fusion.2), kind=kLoop, calls=%fused_computation.1.clone.1 | loop fusion | flops 4161536 | bytes 8650752 | tf_op jit(solution)/shard_map/while/body/eval_jaxpr/reduce_sum | solution.py:48
  143.7 9.0 %copy.20 = f32[4096,512]{1,0:T(8,128)} copy(f32[4096,512]{0,1:T(8,128)} %convolution_bitcast_fusion.4) | data formatting | bytes 16777216 | tf_op jit(solution)/shard_map/while/body/eval_jaxpr/dot_general | solution.py:45
  152.7 4.7 %multiply_reduce_fusion.2 = f32[64,512]{1,0:T(8,128)S(1)} fusion(f32[64,64,512]{2,1,0:T(8,128)} %bitcast.85, f32[64,512]{1,0:T(8,128)S(1)} %bitcast_convert_fusion.2), kind=kLoop, calls=%fused_computation.1.clone.1 | loop fusion | flops 4161536 | bytes 8650752 | tf_op jit(solution)/shard_map/while/body/eval_jaxpr/reduce_sum | solution.py:48
  163.0 9.0 %copy.20 = f32[4096,512]{1,0:T(8,128)} copy(f32[4096,512]{0,1:T(8,128)} %convolution_bitcast_fusion.4) | data formatting | bytes 16777216 | tf_op jit(solution)/shard_map/while/body/eval_jaxpr/dot_general | solution.py:45
  172.0 4.7 %multiply_reduce_fusion.2 = f32[64,512]{1,0:T(8,128)S(1)} fusion(f32[64,64,512]{2,1,0:T(8,128)} %bitcast.85, f32[64,512]{1,0:T(8,128)S(1)} %bitcast_convert_fusion.2), kind=kLoop, calls=%fused_computation.1.clone.1 | loop fusion | flops 4161536 | bytes 8650752 | tf_op jit(solution)/shard_map/while/body/eval_jaxpr/reduce_sum | solution.py:48
  182.2 9.0 %copy.20 = f32[4096,512]{1,0:T(8,128)} copy(f32[4096,512]{0,1:T(8,128)} %convolution_bitcast_fusion.4) | data formatting | bytes 16777216 | tf_op jit(solution)/shard_map/while/body/eval_jaxpr/dot_general | solution.py:45
  191.2 4.7 %multiply_reduce_fusion.2 = f32[64,512]{1,0:T(8,128)S(1)} fusion(f32[64,64,512]{2,1,0:T(8,128)} %bitcast.85, f32[64,512]{1,0:T(8,128)S(1)} %bitcast_convert_fusion.2), kind=kLoop, calls=%fused_computation.1.clone.1 | loop fusion | flops 4161536 | bytes 8650752 | tf_op jit(solution)/shard_map/while/body/eval_jaxpr/reduce_sum | solution.py:48
  201.5 9.0 %copy.20 = f32[4096,512]{1,0:T(8,128)} copy(f32[4096,512]{0,1:T(8,128)} %convolution_bitcast_fusion.4) | data formatting | bytes 16777216 | tf_op jit(solution)/shard_map/while/body/eval_jaxpr/dot_general | solution.py:45
  210.5 4.7 %multiply_reduce_fusion.2 = f32[64,512]{1,0:T(8,128)S(1)} fusion(f32[64,64,512]{2,1,0:T(8,128)} %bitcast.85, f32[64,512]{1,0:T(8,128)S(1)} %bitcast_convert_fusion.2), kind=kLoop, calls=%fused_computation.1.clone.1 | loop fusion | flops 4161536 | bytes 8650752 | tf_op jit(solution)/shard_map/while/body/eval_jaxpr/reduce_sum | solution.py:48
  216.1 19.6 %all_to_all.29 = bf16[8,8,4096]{2,1,0:T(8,128)(2,1)S(1)} all-to-all(bf16[8,8,4096]{2,1,0:T(8,128)(2,1)S(1)} %all_to_all.25), channel_id=1, replica_groups=mesh['sec'=8,'space'=64] {'sec'}, dimensions={0} | all-to-all | bytes 1048576 | tf_op jit(solution)/shard_map/all_to_all | solution.py:78
  (69 shorter events, 60.4 us)
Async XLA Ops:
  0.0 41.6 %copy-start.2 = (f32[64,64]{1,0:T(8,128)S(1)}, f32[64,64]{1,0:T(8,128)}, u32[]{:S(2)}) copy-start(f32[64,64]{1,0:T(8,128)} %param.14) | copy-start | bytes 49156
  0.0 61.3 %copy-start.1 = (bf16[64,64]{1,0:T(8,128)(2,1)S(1)}, bf16[64,64]{1,0:T(8,128)(2,1)}, u32[]{:S(2)}) copy-start(bf16[64,64]{1,0:T(8,128)(2,1)} %param.13) | copy-start | bytes 24580
  0.0 61.4 %copy-start = (s32[64,64]{1,0:T(8,128)S(1)}, s32[64,64]{1,0:T(8,128)}, u32[]{:S(2)}) copy-start(s32[64,64]{1,0:T(8,128)} %param.15) | copy-start | bytes 49156
  1.1 7.7 %collective-permute-start = (f32[8,1,64,128]{3,2,1,0:T(8,128)S(1)}, f32[8,1,64,128]{3,2,1,0:T(8,128)S(1)}, u32[]{:S(2)}, u32[]{:S(2)}) collective-permute-start(f32[8,1,64,128]{3,2,1,0:T(8,128)S(1)} %get-tuple-element.95), channel_id=1, source_target_pairs={{0,1},{1,2},{2,3},{3,4},{4,5},{5,6},{6,7},{7,8},{8,9},{9,10},{10,1... | collective-permute-start | bytes 786440 | tf_op jit(solution)/shard_map/ppermute | solution.py:14
  3.0 8.2 %collective-permute-start.1 = (f32[8,1,64,128]{3,2,1,0:T(8,128)S(1)}, f32[8,1,64,128]{3,2,1,0:T(8,128)S(1)}, u32[]{:S(2)}, u32[]{:S(2)}) collective-permute-start(f32[8,1,64,128]{3,2,1,0:T(8,128)S(1)} %get-tuple-element.96), channel_id=1, source_target_pairs={{1,0},{2,1},{3,2},{4,3},{5,4},{6,5},{7,6},{8,7},{9,8},{10,9},{11,1... | collective-permute-start | bytes 786440 | tf_op jit(solution)/shard_map/ppermute | solution.py:17
  16.4 7.9 %collective-permute-start.2 = (f32[8,1,64,128]{3,2,1,0:T(8,128)S(1)}, f32[8,1,64,128]{3,2,1,0:T(8,128)S(1)}, u32[]{:S(2)}, u32[]{:S(2)}) collective-permute-start(f32[8,1,64,128]{3,2,1,0:T(8,128)S(1)} %get-tuple-element.93), channel_id=1, source_target_pairs={{0,1},{1,2},{2,3},{3,4},{4,5},{5,6},{6,7},{7,8},{8,9},{9,10},{10,1... | collective-permute-start | bytes 786440 | tf_op jit(solution)/shard_map/ppermute | solution.py:14
  19.5 9.3 %collective-permute-start.3 = (f32[8,1,64,128]{3,2,1,0:T(8,128)S(1)}, f32[8,1,64,128]{3,2,1,0:T(8,128)S(1)}, u32[]{:S(2)}, u32[]{:S(2)}) collective-permute-start(f32[8,1,64,128]{3,2,1,0:T(8,128)S(1)} %get-tuple-element.94), channel_id=1, source_target_pairs={{1,0},{2,1},{3,2},{4,3},{5,4},{6,5},{7,6},{8,7},{9,8},{10,9},{11,1... | collective-permute-start | bytes 786440 | tf_op jit(solution)/shard_map/ppermute | solution.py:17
  31.8 29.2 %all-to-all-start = ((bf16[8,8,4096]{2,0,1:T(8,128)(2,1)}), bf16[8,8,4096]{2,0,1:T(8,128)(2,1)S(1)}, u32[]{:S(2)}, u32[]{:S(2)}) async-start(bf16[8,8,4096]{2,0,1:T(8,128)(2,1)} %copy.14), calls=%async_computation | async-start | bytes 1048576 | tf_op jit(solution)/shard_map/all_to_all | solution.py:59
where the time goes:
time: 240 us; the launch traced here: 238 us
  local copies, waits for them, and re-layouts  76.1 us (32%)
  other arithmetic  52.4 us (22%)
  matrix products  38.6 us (16%)
  waiting for transfers between devices  29.7 us (12%)
  starting transfers between devices  21 us (9%)
  blocking collectives  19.6 us (8%)
    dot_general x8, local copies, waits for them, and re-layouts, kinetics(): jnp.dot(pair_table, cells_block, preferred_element_type=jnp.float32)  71.9 us
    reduce_sum x8, other arithmetic, kinetics(): gained = jnp.sum(as_float[:, None, :] * pair_sums, axis=0)  37.6 us
    dot_general x8, matrix products, kinetics(): jnp.dot(pair_table, cells_block, preferred_element_type=jnp.float32)  36.1 us
    all_to_all x1, blocking collectives, per_device(): lax.all_to_all(tendency, 'sec', split_axis=0, concat_axis=1, tiled=True)  19.6 us
    all_to_all x1, waiting for transfers between devices, per_device(): lax.all_to_all(rounded, 'sec', split_axis=1, concat_axis=0, tiled=True)  19.4 us
    all_to_all x1, starting transfers between devices, per_device(): lax.all_to_all(rounded, 'sec', split_axis=1, concat_axis=0, tiled=True)  9.67 us
    ppermute x2, waiting for transfers between devices, with_halo(): lax.ppermute(lax.slice_in_dim(block, 0, width, axis=dim), axis, backward)  6.92 us
    ppermute x2, starting transfers between devices, with_halo(): lax.ppermute(lax.slice_in_dim(block, 0, width, axis=dim), axis, backward)  6.33 us
  transfers between devices with their start and end apart: 5, of which 5 were waited for; matrix products, arithmetic and copies ran while one was open for 0% of the time, Pallas kernels for 0%

commit v1 on v0

v1 whole, which is shorter than its diff:
```python
import functools

import jax
import jax.numpy as jnp
from jax import lax
from jax.experimental import pallas as pl
from jax.experimental.pallas import tpu as pltpu
from jax.sharding import PartitionSpec as P

BF = jnp.bfloat16
F32 = jnp.float32
S = 64
OWN = 8
LAYERS = 4
NY = 64
NZ = 128
HALF = 32
PAIRS = HALF // 2
STEP = 0.25
TABLE_ROWS = 2 * S + sum(8 * (S - 8 * g) for g in range(8))
LIMIT = 48 * 1024 * 1024


def call(body, out_shape, scratch=(), in_specs=None):
    more = {} if in_specs is None else {"in_specs": in_specs}
    return pl.pallas_call(
        body,
        out_shape=out_shape,
        scratch_shapes=scratch,
        compiler_params=pltpu.CompilerParams(vmem_limit_bytes=LIMIT),
        **more,
    )


def strided(x, y):
    return pl.ds(x * NY + y, OWN, stride=LAYERS * NY)


def pack_body(density, wind, low, high):
    def rows(p, _):
        for out, first in ((low, 0), (high, 2)):
            for l in range(2):
                a = density[strided(first + l, 2 * p), :]
                b = density[strided(first + l, 2 * p + 1), :]
                out[l * HALF + p] = jnp.concatenate([a, b], 0).astype(BF)
        return 0

    lax.fori_loop(0, HALF, rows, 0, unroll=4)
    for out, layer in ((low, 0), (high, 3)):
        for t in range(NY // 16):
            out[2 * HALF + t] = wind[layer * NY + 16 * t : layer * NY + 16 * t + 16, :].astype(BF)


def table_body(kernel, target, breakup, table):
    table[0:S, :] = breakup[...]
    table[S : 2 * S, :] = kernel[...].astype(BF)
    base = 2 * S
    for g in range(8):
        low = 8 * g
        count = S - low
        ks = lax.broadcasted_iota(jnp.int32, (count, S), 0) + low
        for i in range(low, low + 8, 2):
            both = [
                jnp.where(target[r : r + 1, :] == ks, kernel[r : r + 1, :], 0.0)
                for r in (i, i + 1)
            ]
            table[base : base + 2 * count, :] = jnp.concatenate(both, 0).astype(BF)
            base += 2 * count


def transport_body(
    inside, density, from_west, from_east, wind, settling, diffusion, field, rounded, old, mid, winds
):
    zero = jnp.zeros((1, OWN, NZ), F32)
    for x in range(LAYERS + 4):
        old[x, 0:1] = zero
        old[x, NY + 1 : NY + 2] = zero
    for x in range(LAYERS + 2):
        mid[x, 0:1] = zero
        mid[x, NY + 1 : NY + 2] = zero

    def bring(p, _):
        for l in range(2):
            for halo, x in ((from_west, l), (from_east, LAYERS + 2 + l)):
                two = halo[l * HALF + p].astype(F32)
                old[x, 2 * p + 1] = two[0:8]
                old[x, 2 * p + 2] = two[8:16]
        for x in range(LAYERS):
            old[x + 2, 2 * p + 1] = density[strided(x, 2 * p), :]
            old[x + 2, 2 * p + 2] = density[strided(x, 2 * p + 1), :]
        return 0

    lax.fori_loop(0, HALF, bring, 0, unroll=2)
    winds[NY : NY + LAYERS * NY, :] = wind[...]
    for t in range(NY // 16):
        winds[16 * t : 16 * t + 16, :] = from_west[2 * HALF + t].astype(F32)
        top = (LAYERS + 1) * NY + 16 * t
        winds[top : top + 16, :] = from_east[2 * HALF + t].astype(F32)

    lane = lax.broadcasted_iota(jnp.int32, (OWN, NZ), 1)
    sink = jnp.broadcast_to(settling[...], (OWN, NZ))
    spread = jnp.broadcast_to(diffusion[...], (OWN, NZ))
    here = 1.0 - sink - 6.0 * spread
    from_above = jnp.where(lane == NZ - 1, 0.0, sink + spread)
    from_below = jnp.where(lane == 0, 0.0, spread)

    def update(ref, x, wind_x, y):
        ten = ref[x, pl.ds(y, 10)]
        c = ten[1:9]
        w = ref[x - 1, pl.ds(y + 1, 8)]
        e = ref[x + 1, pl.ds(y + 1, 8)]
        u = winds[pl.ds(wind_x * NY + y, 8), :]
        u = jnp.broadcast_to(u[:, None, :], (8, OWN, NZ))
        forward = jnp.maximum(u, 0.0)
        backward = jnp.minimum(u, 0.0)
        above = pltpu.roll(c, NZ - 1, 2)
        below = pltpu.roll(c, 1, 2)
        return (
            c * (here - jnp.abs(u))
            + w * (spread + forward)
            + e * (spread - backward)
            + above * from_above
            + below * from_below
            + (ten[0:8] + ten[2:10]) * spread
        )

    def first(b, _):
        y = 8 * b
        for x in range(LAYERS + 2):
            value = update(old, x + 1, x, y)
            if x == 0:
                value = value * inside[0]
            if x == LAYERS + 1:
                value = value * inside[1]
            mid[x, pl.ds(y + 1, 8)] = value
        return 0

    lax.fori_loop(0, NY // 8, first, 0)

    def second(b, _):
        y = 8 * b
        for x in range(LAYERS):
            value = update(mid, x + 1, x + 1, y)
            field[x, pl.ds(y, 8)] = value
            for h in range(4):
                two = jnp.concatenate([value[2 * h], value[2 * h + 1]], 0)
                at = 4 * b + h
                rounded[2 * x + at // PAIRS, lax.rem(at, PAIRS)] = two.astype(BF)
        return 0

    lax.fori_loop(0, NY // 8, second, 0)


def kinetics_body(cells, table, out, wide):
    groups = 2

    def step(q, _):
        parts = []
        for u in range(groups):
            x = cells[:, groups * q + u].astype(F32)
            parts += [x[:, 0:8, :].reshape(S, NZ), x[:, 8:16, :].reshape(S, NZ)]
        n = jnp.concatenate(parts, 1)
        n_bf = n.astype(BF)
        wide[...] = n

        def product(start, stop):
            return jnp.dot(table[start:stop, :], n_bf, preferred_element_type=F32)

        linear = product(0, 2 * S)
        total = linear[0:S] - n * linear[S : 2 * S]
        totals = [total[8 * h : 8 * h + 8] for h in range(8)]
        base = 2 * S
        for g in range(8):
            count = S - 8 * g
            for i in range(8 * g, 8 * g + 8, 2):
                sums = product(base, base + 2 * count)
                base += 2 * count
                at = 0
                for r in (i, i + 1):
                    n_r = wide[r : r + 1, :]
                    for h in range(g, 8):
                        totals[h] = totals[h] + n_r * sums[at : at + 8]
                        at += 8
        total = jnp.concatenate(totals, 0)
        for u in range(groups):
            at = 2 * NZ * u
            a = total[:, at : at + NZ].reshape(8, OWN, NZ)
            b = total[:, at + NZ : at + 2 * NZ].reshape(8, OWN, NZ)
            out[:, groups * q + u] = jnp.concatenate([a, b], 1).astype(BF)
        return 0

    lax.fori_loop(0, PAIRS // groups, step, 0)


def finish_body(field, tendency, out):
    def rows(p, _):
        for x in range(LAYERS):
            for half in range(2):
                y = half * HALF + 2 * p
                two = STEP * tendency[2 * x + half, p].astype(F32)
                out[strided(x, y), :] = field[x, y] + two[0:8]
                out[strided(x, y + 1), :] = field[x, y + 1] + two[8:16]
        return 0

    lax.fori_loop(0, PAIRS, rows, 0, unroll=2)


def per_device(density, wind_speed, settling, diffusion, breakup, coag_kernel, pair_target):
    slabs = lax.axis_size("space")
    me = lax.axis_index("space")
    density = density.reshape(OWN * LAYERS * NY, NZ)
    wind = wind_speed.reshape(LAYERS * NY, NZ)
    forward = [(i, i + 1) for i in range(slabs - 1)]
    backward = [(b, a) for a, b in forward]
    message = jax.ShapeDtypeStruct((2 * HALF + NY // 16, 16, NZ), BF)
    low, high = call(pack_body, (message, message))(density, wind)
    from_west = lax.ppermute(high, "space", forward)
    from_east = lax.ppermute(low, "space", backward)
    table = call(table_body, jax.ShapeDtypeStruct((TABLE_ROWS, S), BF))(
        coag_kernel, pair_target, breakup
    )
    inside = jnp.stack([me > 0, me < slabs - 1]).astype(F32)
    vmem = pl.BlockSpec(memory_space=pltpu.VMEM)
    block = jax.ShapeDtypeStruct((8, PAIRS, 16, NZ), BF)
    field, rounded = call(
        transport_body,
        (jax.ShapeDtypeStruct((LAYERS, NY, OWN, NZ), F32), block),
        scratch=(
            pltpu.VMEM((LAYERS + 4, NY + 2, OWN, NZ), F32),
            pltpu.VMEM((LAYERS + 2, NY + 2, OWN, NZ), F32),
            pltpu.VMEM(((LAYERS + 2) * NY, NZ), F32),
        ),
        in_specs=[pl.BlockSpec(memory_space=pltpu.SMEM)] + [vmem] * 6,
    )(
        inside, density, from_west, from_east, wind,
        settling.reshape(OWN, 1), diffusion.reshape(OWN, 1),
    )
    cells = lax.all_to_all(rounded, "sec", split_axis=0, concat_axis=0, tiled=True)
    tendency = call(kinetics_body, block, scratch=(pltpu.VMEM((S, 4 * NZ), F32),))(cells, table)
    returned = lax.all_to_all(tendency, "sec", split_axis=0, concat_axis=0, tiled=True)
    out = call(finish_body, jax.ShapeDtypeStruct((OWN * LAYERS * NY, NZ), F32))(field, returned)
    return out.reshape(OWN, LAYERS, NY, NZ)


def solution(mesh):
    in_specs = (
        P("sec", "space", None, None),
        P("space", None, None),
        P("sec"),
        P("sec"),
        P(),
        P(),
        P(),
    )
    out_specs = P("sec", "space", None, None)
    return jax.shard_map(
        per_device, mesh=mesh, in_specs=in_specs, out_specs=out_specs, check_vma=False
    )
```

time: 240 us -> 75.5 us (0.31)
  the two profiles are of different devices: /device:TPU:336 before, /device:TPU:400 now
where the time goes in v1:
time: 75.5 us; the launch traced here: 75.1 us
  waiting for transfers between devices  22.7 us (30%)
  blocking collectives  19.7 us (26%)
  starting transfers between devices  15.3 us (20%)
  Pallas kernels  13.6 us (18%)
  local copies, waits for them, and re-layouts  3.61 us (5%)
    all_to_all x1, blocking collectives, per_device(): lax.all_to_all(tendency, 'sec', split_axis=0, concat_axis=0, tiled=True)  19.7 us
    all_to_all x1, waiting for transfers between devices, per_device(): lax.all_to_all(rounded, 'sec', split_axis=0, concat_axis=0, tiled=True)  19.4 us
    all_to_all x1, starting transfers between devices, per_device(): lax.all_to_all(rounded, 'sec', split_axis=0, concat_axis=0, tiled=True)  9.73 us
    pallas_call x1, Pallas kernels, per_device(): call(kinetics_body, block, scratch=(pltpu.VMEM((S, 4 * NZ), F32),))  6.46 us
    pallas_call x1, Pallas kernels, per_device(): call(transport_body, (jax.ShapeDtypeStruct((LAYERS, NY, OWN, NZ), F32), b...  4.66 us
    ppermute x1, starting transfers between devices, per_device(): from_east = lax.ppermute(low, 'space', backward)  3.64 us
    unnamed x18, local copies, waits for them, and re-layouts  3.45 us
    ppermute x1, waiting for transfers between devices, per_device(): from_east = lax.ppermute(low, 'space', backward)  2.65 us
  transfers between devices with their start and end apart: 3, of which 3 were waited for; matrix products, arithmetic and copies ran while one was open for 0% of the time, Pallas kernels for 0%

profile of v1, /device:TPU:400, one launch (start us, length us, event | category | flops | bytes accessed | tf_op | source)
XLA Modules:
  0.0 75.1 jit_solution(5258814340577472808)
XLA Ops:
  0.0 1.2 %copy-done = f32[8,4,64,128]{3,2,1,0:T(8,128)S(1)} copy-done((f32[8,4,64,128]{3,2,1,0:T(8,128)S(1)}, f32[8,4,64,128]{3,2,1,0:T(8,128)}, u32[]{:S(2)}) %copy-start) | copy-done | bytes 1048600
  1.2 0.9 %copy-done.2 = f32[4,64,128]{2,1,0:T(8,128)S(1)} copy-done((f32[4,64,128]{2,1,0:T(8,128)S(1)}, f32[4,64,128]{2,1,0:T(8,128)}, u32[]{:S(2)}) %copy-start.2) | copy-done | bytes 131096
  2.1 0.6 shard_map.73
  2.8 1.9 %collective-permute-start = (bf16[68,16,128]{2,1,0:T(8,128)(2,1)S(1)}, bf16[68,16,128]{2,1,0:T(8,128)(2,1)S(1)}, u32[]{:S(2)}, u32[]{:S(2)}) collective-permute-start(bf16[68,16,128]{2,1,0:T(8,128)(2,1)S(1)} %get-tuple-element.9), channel_id=1, source_target_pairs={{0,1},{1,2},{2,3},{3,4},{4,5},{5,6},{6,7},{7,8},{8,9},{9,10},{10,1... | collective-permute-start | bytes 835592 | tf_op jit(solution)/shard_map/ppermute | solution.py:217
  4.7 3.6 %collective-permute-start.1 = (bf16[68,16,128]{2,1,0:T(8,128)(2,1)S(1)}, bf16[68,16,128]{2,1,0:T(8,128)(2,1)S(1)}, u32[]{:S(2)}, u32[]{:S(2)}) collective-permute-start(bf16[68,16,128]{2,1,0:T(8,128)(2,1)S(1)} %get-tuple-element.10), channel_id=1, source_target_pairs={{1,0},{2,1},{3,2},{4,3},{5,4},{6,5},{7,6},{8,7},{9,8},{10,9},{11,1... | collective-permute-start | bytes 835592 | tf_op jit(solution)/shard_map/ppermute | solution.py:218
  8.3 0.0 copy-start.7
  8.4 0.6 copy-done.7
  9.0 0.1 copy.8.settling
  9.1 0.7 copy-done.8
  9.7 0.1 copy.9.diffusion
  9.8 0.1 add_convert_fusion.inside
  9.9 0.7 collective-permute-done.from_west
  10.6 2.6 %collective-permute-done.1.from_east = bf16[68,16,128]{2,1,0:T(8,128)(2,1)S(1)} collective-permute-done((bf16[68,16,128]{2,1,0:T(8,128)(2,1)S(1)}, bf16[68,16,128]{2,1,0:T(8,128)(2,1)S(1)}, u32[]{:S(2)}, u32[]{:S(2)}) %collective-permute-start.1) | collective-permute-done | bytes 278560 | tf_op jit(solution)/shard_map/ppermute | solution.py:218
  13.3 0.0 copy-done.1
  13.3 0.0 copy-done.3
  13.3 4.7 %shard_map.74 = (f32[4,64,8,128]{3,2,1,0:T(8,128)S(1)}, bf16[8,16,16,128]{3,2,1,0:T(8,128)(2,1)}) custom-call(f32[2]{0:T(128)S(1)} %add_convert_fusion.inside, f32[2048,128]{1,0:T(8,128)S(1)} %bitcast.8, bf16[68,16,128]{2,1,0:T(8,128)(2,1)S(1)} %collective-permute-done.from_west, bf16[68,16,128]{2,1,0:T(8,128)(2,1)S(1)} %collective-permute-done.1.from_east, ...), custom_call_target="tpu_custom_call" | custom-call | tf_op jit(solution)/shard_map/pallas_call | solution.py:225
  18.0 9.7 %all-to-all-start = ((bf16[8,16,16,128]{3,2,1,0:T(8,128)(2,1)}), bf16[8,16,16,128]{3,2,1,0:T(8,128)(2,1)S(1)}, u32[]{:S(2)}, u32[]{:S(2)}) async-start(bf16[8,16,16,128]{3,2,1,0:T(8,128)(2,1)} %get-tuple-element.12), calls=%async_computation | async-start | bytes 1048576 | tf_op jit(solution)/shard_map/all_to_all | solution.py:238
  27.7 0.0 copy-done.4
  27.7 0.0 copy-done.5
  27.7 0.1 shard_map.75.table
  27.8 19.4 %all-to-all-done.cells = bf16[8,16,16,128]{3,2,1,0:T(8,128)(2,1)S(1)} async-done(((bf16[8,16,16,128]{3,2,1,0:T(8,128)(2,1)}), bf16[8,16,16,128]{3,2,1,0:T(8,128)(2,1)S(1)}, u32[]{:S(2)}, u32[]{:S(2)}) %all-to-all-start) | async-done | bytes 524320 | tf_op jit(solution)/shard_map/all_to_all | solution.py:238
  47.2 6.5 %shard_map.76 = bf16[8,16,16,128]{3,2,1,0:T(8,128)(2,1)S(1)} custom-call(bf16[8,16,16,128]{3,2,1,0:T(8,128)(2,1)S(1)} %all-to-all-done.cells, bf16[2432,64]{1,0:T(8,128)(2,1)S(1)} %shard_map.75.table), custom_call_target="tpu_custom_call" | custom-call | tf_op jit(solution)/shard_map/pallas_call | solution.py:239
  53.7 19.7 %all_to_all.10.tendency = bf16[8,16,16,128]{3,2,1,0:T(8,128)(2,1)S(1)} all-to-all(bf16[8,16,16,128]{3,2,1,0:T(8,128)(2,1)S(1)} %shard_map.76), channel_id=1, replica_groups=mesh['sec'=8,'space'=64] {'sec'}, dimensions={0} | all-to-all | bytes 1048576 | tf_op jit(solution)/shard_map/all_to_all | solution.py:240
  73.3 1.7 %shard_map.77 = f32[2048,128]{1,0:T(8,128)} custom-call(f32[4,64,8,128]{3,2,1,0:T(8,128)S(1)} %get-tuple-element.11.field, bf16[8,16,16,128]{3,2,1,0:T(8,128)(2,1)S(1)} %all_to_all.10.tendency), custom_call_target="tpu_custom_call" | custom-call | tf_op jit(solution)/shard_map/pallas_call | solution.py:241
  (9 shorter events, 0.0 us)
Async XLA Ops:
  0.0 1.2 %copy-start = (f32[8,4,64,128]{3,2,1,0:T(8,128)S(1)}, f32[8,4,64,128]{3,2,1,0:T(8,128)}, u32[]{:S(2)}) copy-start(f32[8,4,64,128]{3,2,1,0:T(8,128)} %param.7) | copy-start | bytes 3145732
  1.2 0.9 %copy-start.2 = (f32[4,64,128]{2,1,0:T(8,128)S(1)}, f32[4,64,128]{2,1,0:T(8,128)}, u32[]{:S(2)}) copy-start(f32[4,64,128]{2,1,0:T(8,128)} %param.8) | copy-start | bytes 393220
  2.1 11.1 %copy-start.1 = (f32[8,4,64,128]{3,2,1,0:T(8,128)S(1)}, f32[8,4,64,128]{3,2,1,0:T(8,128)}, u32[]{:S(2)}) copy-start(f32[8,4,64,128]{3,2,1,0:T(8,128)} %param.7) | copy-start | bytes 3145732
  2.1 11.1 %copy-start.3 = (f32[4,64,128]{2,1,0:T(8,128)S(1)}, f32[4,64,128]{2,1,0:T(8,128)}, u32[]{:S(2)}) copy-start(f32[4,64,128]{2,1,0:T(8,128)} %param.8) | copy-start | bytes 393220
  2.8 7.9 %collective-permute-start = (bf16[68,16,128]{2,1,0:T(8,128)(2,1)S(1)}, bf16[68,16,128]{2,1,0:T(8,128)(2,1)S(1)}, u32[]{:S(2)}, u32[]{:S(2)}) collective-permute-start(bf16[68,16,128]{2,1,0:T(8,128)(2,1)S(1)} %get-tuple-element.9), channel_id=1, source_target_pairs={{0,1},{1,2},{2,3},{3,4},{4,5},{5,6},{6,7},{7,8},{8,9},{9,10},{10,1... | collective-permute-start | bytes 835592 | tf_op jit(solution)/shard_map/ppermute | solution.py:217
  4.7 8.6 %collective-permute-start.1 = (bf16[68,16,128]{2,1,0:T(8,128)(2,1)S(1)}, bf16[68,16,128]{2,1,0:T(8,128)(2,1)S(1)}, u32[]{:S(2)}, u32[]{:S(2)}) collective-permute-start(bf16[68,16,128]{2,1,0:T(8,128)(2,1)S(1)} %get-tuple-element.10), channel_id=1, source_target_pairs={{1,0},{2,1},{3,2},{4,3},{5,4},{6,5},{7,6},{8,7},{9,8},{10,9},{11,1... | collective-permute-start | bytes 835592 | tf_op jit(solution)/shard_map/ppermute | solution.py:218
  8.3 0.7 copy-start.7
  9.1 0.7 copy-start.8
  17.9 9.7 %copy-start.4 = (f32[64,64]{1,0:T(8,128)S(1)}, f32[64,64]{1,0:T(8,128)}, u32[]{:S(2)}) copy-start(f32[64,64]{1,0:T(8,128)} %kernel.1) | copy-start | bytes 49156
  17.9 9.7 %copy-start.5 = (s32[64,64]{1,0:T(8,128)S(1)}, s32[64,64]{1,0:T(8,128)}, u32[]{:S(2)}) copy-start(s32[64,64]{1,0:T(8,128)} %target.1) | copy-start | bytes 49156
  18.0 9.7 %copy-start.6 = (bf16[64,64]{1,0:T(8,128)(2,1)S(1)}, bf16[64,64]{1,0:T(8,128)(2,1)}, u32[]{:S(2)}) copy-start(bf16[64,64]{1,0:T(8,128)(2,1)} %breakup.1) | copy-start | bytes 24580
  18.0 29.3 %all-to-all-start = ((bf16[8,16,16,128]{3,2,1,0:T(8,128)(2,1)}), bf16[8,16,16,128]{3,2,1,0:T(8,128)(2,1)S(1)}, u32[]{:S(2)}, u32[]{:S(2)}) async-start(bf16[8,16,16,128]{3,2,1,0:T(8,128)(2,1)} %get-tuple-element.12), calls=%async_computation | async-start | bytes 1048576 | tf_op jit(solution)/shard_map/all_to_all | solution.py:238

commit v2 on v0

v2 whole, which is shorter than its diff:
```python
import jax
import jax.numpy as jnp
from jax import lax
from jax.experimental import pallas as pl
from jax.experimental.pallas import tpu as pltpu
from jax.sharding import PartitionSpec as P

BF = jnp.bfloat16
F32 = jnp.float32
S = 64
OWN = 8
LAYERS = 4
NY = 64
NZ = 128
HALF = 32
PAIRS = HALF // 2
STEP = 0.25
PAIR_ROWS = sum(8 * (S - 8 * g) for g in range(8))
LIMIT = 48 * 1024 * 1024


def call(body, out_shape, scratch=(), **specs):
    return pl.pallas_call(
        body,
        out_shape=out_shape,
        scratch_shapes=scratch,
        compiler_params=pltpu.CompilerParams(vmem_limit_bytes=LIMIT),
        **specs,
    )


def bring_layer(loaded, out, x):
    zero = jnp.zeros((1, OWN, NZ), F32)
    out[x, 0:1] = zero
    out[x, NY + 1 : NY + 2] = zero

    def rows(p, _):
        for r in range(8):
            out[x, 8 * p + r + 1] = loaded[pl.ds(8 * p + r, OWN, stride=NY), :]
        return 0

    lax.fori_loop(0, NY // 8, rows, 0, unroll=True)


def pack_layer(layer, x, out, at):
    def rows(p, _):
        for r in range(4):
            two = layer[x, pl.ds(8 * p + 2 * r + 1, 2)].reshape(16, NZ)
            out[at + 4 * p + r] = two.astype(BF)
        return 0

    lax.fori_loop(0, NY // 8, rows, 0, unroll=True)


def pack_body(flags, density, wind, out, old, loaded, windy, sems):
    base = flags[0]
    copies = [
        pltpu.make_async_copy(density.at[:, base], loaded.at[0], sems.at[0]),
        pltpu.make_async_copy(density.at[:, base + 1], loaded.at[1], sems.at[1]),
        pltpu.make_async_copy(wind.at[flags[1]], windy, sems.at[2]),
    ]
    for copy in copies:
        copy.start()
    for l in range(2):
        copies[l].wait()
        bring_layer(loaded.at[l].reshape(OWN * NY, NZ), old, l)
        pack_layer(old, l, out, l * HALF)
    copies[2].wait()
    for t in range(NY // 16):
        out[2 * HALF + t] = windy[16 * t : 16 * t + 16, :].astype(BF)


def table_body(kernel, target, breakup, linear, pairs, columns):
    linear[0:S, :] = breakup[...]
    linear[S : 2 * S, :] = kernel[...].astype(BF)
    rates = kernel[...].astype(BF).astype(F32)
    rates_t = jnp.transpose(rates)
    target_t = jnp.transpose(target[...])
    base = 0
    for g in range(8):
        low = 8 * g
        count = S - low
        ks = lax.broadcasted_iota(jnp.int32, (count, S), 1)
        js = lax.broadcasted_iota(jnp.int32, (count, S), 0) + low
        for i in range(low, low + 8):
            one = jnp.where((target_t[low:, i : i + 1] == ks) & (js >= i), rates_t[low:, i : i + 1], 0.0)
            two = jnp.where((target[low:, i : i + 1] == ks) & (js > i), rates[low:, i : i + 1], 0.0)
            columns[base : base + count, 0:S] = one + two
            base += count
    for t in range(PAIR_ROWS // NZ):
        pairs[:, t * NZ : (t + 1) * NZ] = jnp.transpose(columns[t * NZ : (t + 1) * NZ, :])[0:S, :].astype(BF)


def spread_rows(rows):
    return jnp.broadcast_to(rows[:, None, :], (8, OWN, NZ))


def within(ten, u, constants):
    here, from_above, from_below, spread = constants
    c = ten[1:9]
    return (
        c * (here - jnp.abs(u))
        + pltpu.roll(c, NZ - 1, 2) * from_above
        + pltpu.roll(c, 1, 2) * from_below
        + (ten[0:8] + ten[2:10]) * spread
    )


def from_west_of(u, spread):
    return spread + jnp.maximum(u, 0.0)


def from_east_of(u, spread):
    return spread - jnp.minimum(u, 0.0)


def per_section(ref):
    row = lax.broadcasted_iota(jnp.int32, (OWN, NZ), 0)
    out = jnp.zeros((OWN, NZ), F32)
    for s in range(OWN):
        out = jnp.where(row == s, ref[s], out)
    return out


def inner_body(
    flags, settling, diffusion, sent, kept, wind, kernel, target, breakup,
    old, field, reach, constants, linear, pairs, mid, columns,
):
    table_body(kernel, target, breakup, linear, pairs, columns)
    sink, spread = per_section(settling), per_section(diffusion)
    lane = lax.broadcasted_iota(jnp.int32, (OWN, NZ), 1)
    held = (
        1.0 - sink - 6.0 * spread,
        jnp.where(lane == NZ - 1, 0.0, sink + spread),
        jnp.where(lane == 0, 0.0, spread),
        spread,
    )
    for i in range(4):
        constants[i] = held[i]
    zero = jnp.zeros((1, OWN, NZ), F32)
    for x in range(LAYERS):
        mid[x, 0:1] = zero
        mid[x, NY + 1 : NY + 2] = zero

    @pl.when(flags[0] == 0)
    def _():
        for l in range(2):
            old[l] = sent[l]
            old[2 + l] = kept[l]

    @pl.when(flags[0] != 0)
    def _():
        for l in range(2):
            old[l] = kept[l]
            old[2 + l] = sent[l]

    def substep(ref, y, store, store_reach=None):
        for x in range(LAYERS):
            u = spread_rows(wind[x, pl.ds(y, 8), :])
            west, east = from_west_of(u, spread), from_east_of(u, spread)
            value = within(ref[x, pl.ds(y, 10)], u, held)
            if x > 0:
                value = value + ref[x - 1, pl.ds(y + 1, 8)] * west
            if x < LAYERS - 1:
                value = value + ref[x + 1, pl.ds(y + 1, 8)] * east
            store(x, value)
            if store_reach is not None:
                store_reach(x, west if x < 2 else east)

    def first(b, _):
        y = pl.multiple_of(8 * b, 8)

        def store(x, value):
            mid[x, pl.ds(y + 1, 8)] = value

        def store_reach(x, value):
            reach[x, pl.ds(y, 8)] = value

        substep(old, y, store, store_reach)
        return 0

    def second(b, _):
        y = pl.multiple_of(8 * b, 8)

        def store(x, value):
            field[x, pl.ds(y, 8)] = value

        substep(mid, y, store)
        return 0

    lax.fori_loop(0, NY // 8, first, 0, unroll=True)
    lax.fori_loop(0, NY // 8, second, 0, unroll=True)


def outer_body(
    flags, partner, other, wind, old, inner, reach, constants, field, rounded, halo, change, beyond
):
    odd = flags[0]
    held = tuple(constants[i] for i in range(4))
    spread = held[3]
    zero = jnp.zeros((1, OWN, NZ), F32)
    for side in range(2):
        for ref in (halo, change):
            ref[side, 0:1] = zero
            ref[side, NY + 1 : NY + 2] = zero
    sides = ((partner, 1 - odd), (other, odd))

    def bring(p, _):
        for message, side in sides:
            for r in range(4):
                two = message[(1 - side) * HALF + 4 * p + r].astype(F32).reshape(2, OWN, NZ)
                halo[side, pl.ds(8 * p + 2 * r + 1, 2)] = two
        return 0

    lax.fori_loop(0, NY // 8, bring, 0, unroll=True)

    def through(b, _):
        y = pl.multiple_of(8 * b, 8)
        for message, side in sides:
            edge = 3 * side
            sign = 1.0 - 2.0 * side.astype(F32)
            inside = flags[1 + side].astype(F32)
            far = [
                message[side * HALF + 4 * b + h].astype(F32).reshape(2, OWN, NZ) for h in range(4)
            ]
            far = jnp.concatenate(far, 0)
            winds = message[2 * HALF + b // 2].astype(F32)
            u = spread_rows(jnp.where(lax.rem(b, 2) == 0, winds[0:8], winds[8:16]))
            outward = sign * u
            ten = halo[side, pl.ds(y, 10)]
            value = (
                within(ten, u, held)
                + far * (spread + jnp.maximum(outward, 0.0))
                + old[edge, pl.ds(y + 1, 8)] * (spread - jnp.minimum(outward, 0.0))
            )
            beyond[side, pl.ds(y, 8)] = value * inside
            change[side, pl.ds(y + 1, 8)] = ten[1:9] * reach[edge, pl.ds(y, 8)]
        return 0

    lax.fori_loop(0, NY // 8, through, 0, unroll=True)

    def finish(b, _):
        y = pl.multiple_of(8 * b, 8)
        for x in range(LAYERS):
            side = x // 2
            r = reach[x, pl.ds(y, 8)]
            value = inner[x, pl.ds(y, 8)]
            if x in (0, LAYERS - 1):
                u = spread_rows(wind[x, pl.ds(y, 8), :])
                ten = change[side, pl.ds(y, 10)]
                value = value + within(ten, u, held) + beyond[side, pl.ds(y, 8)] * r
            else:
                value = value + change[side, pl.ds(y + 1, 8)] * r
            field[x, pl.ds(y, 8)] = value
            for h in range(4):
                two = value[2 * h : 2 * h + 2].reshape(16, NZ)
                at = 4 * b + h
                rounded[2 * x + at // PAIRS, lax.rem(at, PAIRS)] = two.astype(BF)
        return 0

    lax.fori_loop(0, NY // 8, finish, 0, unroll=True)


WIDE = 4


def kinetics_body(cells, linear, pairs, out, wide, products):
    def step(q, _):
        parts = []
        for u in range(WIDE):
            x = cells[:, WIDE * q + u].astype(F32)
            parts += [x[:, 0:8, :].reshape(S, NZ), x[:, 8:16, :].reshape(S, NZ)]
        n = jnp.concatenate(parts, 1)
        wide[...] = n
        base = 0
        for g in range(8):
            count = S - 8 * g
            high = n[8 * g :]
            for i in range(8 * g, 8 * g + 8, 2):
                both = [high * wide[r : r + 1, :] for r in (i, i + 1)]
                products[base : base + 2 * count, :] = jnp.concatenate(both, 0).astype(BF)
                base += 2 * count
        gained = jnp.dot(pairs[...], products[...], preferred_element_type=F32)
        straight = jnp.dot(linear[...], n.astype(BF), preferred_element_type=F32)
        total = straight[0:S] + gained - n * straight[S : 2 * S]
        for u in range(WIDE):
            at = 2 * NZ * u
            a = total[:, at : at + NZ].reshape(8, OWN, NZ)
            b = total[:, at + NZ : at + 2 * NZ].reshape(8, OWN, NZ)
            out[:, WIDE * q + u] = jnp.concatenate([a, b], 1).astype(BF)
        return 0

    lax.fori_loop(0, PAIRS // WIDE, step, 0)


def finish_body(field, tendency, out, held, sems):
    copies = []
    for x in range(LAYERS):
        layer = held.at[x].reshape(OWN * NY, NZ)

        def rows(p, _):
            for half in range(2):
                y = half * HALF + 2 * p
                two = STEP * tendency[2 * x + half, p].astype(F32)
                layer[pl.ds(y, OWN, stride=NY), :] = field[x, y] + two[0:8]
                layer[pl.ds(y + 1, OWN, stride=NY), :] = field[x, y + 1] + two[8:16]
            return 0

        lax.fori_loop(0, PAIRS, rows, 0, unroll=True)
        copies.append(pltpu.make_async_copy(held.at[x], out.at[:, x], sems.at[x]))
        copies[x].start()
    for copy in copies:
        copy.wait()


def per_device(density, wind_speed, settling, diffusion, breakup, coag_kernel, pair_target):
    slabs = lax.axis_size("space")
    me = lax.axis_index("space")
    odd = me % 2
    flags = jnp.stack([odd, (me > 0).astype(jnp.int32), (me < slabs - 1).astype(jnp.int32)])
    smem = pl.BlockSpec(memory_space=pltpu.SMEM)
    vmem = pl.BlockSpec(memory_space=pltpu.VMEM)
    hbm = pl.BlockSpec(memory_space=pltpu.HBM)
    message = jax.ShapeDtypeStruct((2 * HALF + NY // 16, 16, NZ), BF)
    block = jax.ShapeDtypeStruct((8, PAIRS, 16, NZ), BF)
    cells_f32 = jax.ShapeDtypeStruct((LAYERS, NY, OWN, NZ), F32)
    padded = (LAYERS, NY + 2, OWN, NZ)

    def pack(first_layer, edge):
        return call(
            pack_body,
            (message, jax.ShapeDtypeStruct((2, NY + 2, OWN, NZ), F32)),
            scratch=(
                pltpu.VMEM((2, OWN, NY, NZ), F32),
                pltpu.VMEM((NY, NZ), F32),
                pltpu.SemaphoreType.DMA((3,)),
            ),
            in_specs=[smem, hbm, hbm],
        )(jnp.stack([first_layer, edge]), density, wind_speed)

    to_other, sent = pack(2 * odd, 3 * odd)
    other = lax.ppermute(to_other, "space", [(i, ((i + 1) ^ 1) - 1) for i in range(1, slabs - 1)])
    to_partner, kept = pack(2 - 2 * odd, 3 - 3 * odd)
    partner = lax.ppermute(to_partner, "space", [(i, i ^ 1) for i in range(slabs)])
    old, inner, reach, constants, linear, pairs = call(
        inner_body,
        (
            jax.ShapeDtypeStruct(padded, F32),
            cells_f32,
            cells_f32,
            jax.ShapeDtypeStruct((4, OWN, NZ), F32),
            jax.ShapeDtypeStruct((2 * S, S), BF),
            jax.ShapeDtypeStruct((S, PAIR_ROWS), BF),
        ),
        scratch=(pltpu.VMEM(padded, F32), pltpu.VMEM((PAIR_ROWS, NZ), F32)),
        in_specs=[smem] * 3 + [vmem] * 6,
    )(flags, settling, diffusion, sent, kept, wind_speed, coag_kernel, pair_target, breakup)
    field, rounded = call(
        outer_body,
        (cells_f32, block),
        scratch=(
            pltpu.VMEM((2, NY + 2, OWN, NZ), F32),
            pltpu.VMEM((2, NY + 2, OWN, NZ), F32),
            pltpu.VMEM((2, NY, OWN, NZ), F32),
        ),
        in_specs=[smem] + [vmem] * 7,
    )(flags, partner, other, wind_speed, old, inner, reach, constants)
    cells = lax.all_to_all(rounded, "sec", split_axis=0, concat_axis=0, tiled=True)
    width = 2 * NZ * WIDE
    tendency = call(
        kinetics_body,
        block,
        scratch=(pltpu.VMEM((S, width), F32), pltpu.VMEM((PAIR_ROWS, width), BF)),
    )(cells, linear, pairs)
    returned = lax.all_to_all(tendency, "sec", split_axis=0, concat_axis=0, tiled=True)
    return call(
        finish_body,
        jax.ShapeDtypeStruct((OWN, LAYERS, NY, NZ), F32),
        scratch=(pltpu.VMEM((LAYERS, OWN, NY, NZ), F32), pltpu.SemaphoreType.DMA((LAYERS,))),
        in_specs=[vmem, vmem],
        out_specs=hbm,
    )(field, returned)


def solution(mesh):
    in_specs = (
        P("sec", "space", None, None),
        P("space", None, None),
        P("sec"),
        P("sec"),
        P(),
        P(),
        P(),
    )
    out_specs = P("sec", "space", None, None)
    return jax.shard_map(
        per_device, mesh=mesh, in_specs=in_specs, out_specs=out_specs, check_vma=False
    )
```

time: 240 us -> 67.5 us (0.28)
  the two profiles are of different devices: /device:TPU:336 before, /device:TPU:216 now
where the time goes in v2:
time: 67.5 us; the launch traced here: 67.2 us
  blocking collectives  45.1 us (67%)
  Pallas kernels  12.5 us (19%)
  starting transfers between devices  7.17 us (11%)
  local copies, waits for them, and re-layouts  2.16 us (3%)
    all_to_all x1, blocking collectives, per_device(): lax.all_to_all(rounded, 'sec', split_axis=0, concat_axis=0, tiled=True)  23.9 us
    all_to_all x1, blocking collectives, per_device(): lax.all_to_all(tendency, 'sec', split_axis=0, concat_axis=0, tiled=True)  21.2 us
    ppermute x1, starting transfers between devices, per_device(): lax.ppermute(to_partner, 'space', [(i, i ^ 1) for i in range(slabs)])  5.25 us
    pallas_call x1, Pallas kernels, per_device(): call(kinetics_body, block, scratch=(pltpu.VMEM((S, width), F32), pltpu.VM...  4.22 us
    pallas_call x1, Pallas kernels, per_device(): call(inner_body, (jax.ShapeDtypeStruct(padded, F32), cells_f32, cells_f32...  3.26 us
    unnamed x18, local copies, waits for them, and re-layouts  2.16 us
    pallas_call x2, Pallas kernels, pack(): call(pack_body, (message, jax.ShapeDtypeStruct((2, NY + 2, OWN, NZ), F32)...  1.96 us
    ppermute x1, starting transfers between devices, per_device(): lax.ppermute(to_other, 'space', [(i, (i + 1 ^ 1) - 1) for i in range(1, s...  1.92 us
  transfers between devices with their start and end apart: 2, of which 0 were waited for; matrix products, arithmetic and copies ran while one was open for 0% of the time, Pallas kernels for 6%

profile of v2, /device:TPU:216, one launch (start us, length us, event | category | flops | bytes accessed | tf_op | source)
XLA Modules:
  0.0 67.2 jit_solution(9738718044402915128)
XLA Ops:
  0.0 0.1 pad_add_fusion.2.flags
  0.1 1.2 %copy-done = f32[8,4,64,128]{3,2,1,0:T(8,128)S(1)} copy-done((f32[8,4,64,128]{3,2,1,0:T(8,128)S(1)}, f32[8,4,64,128]{3,2,1,0:T(8,128)}, u32[]{:S(2)}) %copy-start) | copy-done | bytes 1048600
  1.3 0.9 %copy-done.2 = f32[4,64,128]{2,1,0:T(8,128)S(1)} copy-done((f32[4,64,128]{2,1,0:T(8,128)S(1)}, f32[4,64,128]{2,1,0:T(8,128)}, u32[]{:S(2)}) %copy-start.2) | copy-done | bytes 131096
  2.2 0.0 copy-start.6
  2.2 0.0 copy-start.7
  2.2 0.0 copy-start.8
  2.3 1.0 %shard_map.74 = (bf16[68,16,128]{2,1,0:T(8,128)(2,1)S(1)}, f32[2,66,8,128]{3,2,1,0:T(8,128)S(1)}) custom-call(s32[2]{0:T(128)S(1)} %pad_add_fusion.2.flags, f32[8,4,64,128]{3,2,1,0:T(8,128)S(1)} %copy-done, f32[4,64,128]{2,1,0:T(8,128)S(1)} %copy-done.2), custom_call_target="tpu_custom_call" | custom-call | tf_op jit(solution)/shard_map/pallas_call | solution.py:330
  3.2 1.9 %collective-permute-start.1 = (bf16[68,16,128]{2,1,0:T(8,128)(2,1)S(1)}, bf16[68,16,128]{2,1,0:T(8,128)(2,1)S(1)}, u32[]{:S(2)}, u32[]{:S(2)}) collective-permute-start(bf16[68,16,128]{2,1,0:T(8,128)(2,1)S(1)} %get-tuple-element.18), channel_id=1, source_target_pairs={{1,2},{2,1},{3,4},{4,3},{5,6},{6,5},{7,8},{8,7},{9,10},{10,9},{11,... | collective-permute-start | bytes 835592 | tf_op jit(solution)/shard_map/ppermute | solution.py:342
  5.2 0.1 pad_add_fusion.1.flags
  5.3 0.0 copy-done.1
  5.3 0.0 copy-done.3
  5.3 1.0 %shard_map.73 = (bf16[68,16,128]{2,1,0:T(8,128)(2,1)S(1)}, f32[2,66,8,128]{3,2,1,0:T(8,128)S(1)}) custom-call(s32[2]{0:T(128)S(1)} %pad_add_fusion.1.flags, f32[8,4,64,128]{3,2,1,0:T(8,128)S(1)} %copy-done.1, f32[4,64,128]{2,1,0:T(8,128)S(1)} %copy-done.3), custom_call_target="tpu_custom_call" | custom-call | tf_op jit(solution)/shard_map/pallas_call | solution.py:330
  6.2 5.3 %collective-permute-start = (bf16[68,16,128]{2,1,0:T(8,128)(2,1)S(1)}, bf16[68,16,128]{2,1,0:T(8,128)(2,1)S(1)}, u32[]{:S(2)}, u32[]{:S(2)}) collective-permute-start(bf16[68,16,128]{2,1,0:T(8,128)(2,1)S(1)} %get-tuple-element.17), channel_id=1, source_target_pairs={{0,1},{1,0},{2,3},{3,2},{4,5},{5,4},{6,7},{7,6},{8,9},{9,8},{10,11... | collective-permute-start | bytes 835592 | tf_op jit(solution)/shard_map/ppermute | solution.py:344
  11.5 0.1 pad_add_fusion.flags
  11.6 0.0 copy-done.4
  11.6 0.0 copy-done.5
  11.6 3.3 %shard_map.75 = (f32[4,66,8,128]{3,2,1,0:T(8,128)S(1)}, f32[4,64,8,128]{3,2,1,0:T(8,128)S(1)}, f32[4,64,8,128]{3,2,1,0:T(8,128)S(1)}, f32[4,8,128]{2,1,0:T(8,128...) custom-call(s32[3]{0:T(128)S(1)} %pad_add_fusion.flags, f32[8]{0:T(128)S(1)} %copy-done.7, ...), custom_call_target="tpu_custom_call" | custom-call | tf_op jit(solution)/shard_map/pallas_call | solution.py:345
  14.9 0.0 collective-permute-done.1.other
  14.9 0.0 collective-permute-done.partner
  14.9 1.5 %shard_map.76 = (f32[4,64,8,128]{3,2,1,0:T(8,128)S(1)}, bf16[8,16,16,128]{3,2,1,0:T(8,128)(2,1)S(1)}) custom-call(s32[3]{0:T(128)S(1)} %pad_add_fusion.flags, bf16[68,16,128]{2,1,0:T(8,128)(2,1)S(1)} %collective-permute-done.partner, bf16[68,16,128]{2,1,0:T(8,128)(2,1)S(1)} %collective-permute-done.1.other, f32[4,64,128]{2,1,0:T(8,128)S(1)} %copy-done.3, ...), custom_call_target="tpu_custom_call" | custom-call | tf_op jit(solution)/shard_map/pallas_call | solution.py:358
  16.4 23.9 %all_to_all.10.cells = bf16[8,16,16,128]{3,2,1,0:T(8,128)(2,1)S(1)} all-to-all(bf16[8,16,16,128]{3,2,1,0:T(8,128)(2,1)S(1)} %get-tuple-element.26), channel_id=1, replica_groups=mesh['sec'=8,'space'=64] {'sec'}, dimensions={0} | all-to-all | bytes 1048576 | tf_op jit(solution)/shard_map/all_to_all | solution.py:368
  40.3 4.2 %shard_map.77 = bf16[8,16,16,128]{3,2,1,0:T(8,128)(2,1)S(1)} custom-call(bf16[8,16,16,128]{3,2,1,0:T(8,128)(2,1)S(1)} %all_to_all.10.cells, bf16[128,64]{1,0:T(8,128)(2,1)S(1)} %get-tuple-element.27.linear, bf16[64,2304]{1,0:T(8,128)(2,1)S(1)} %get-tuple-element.28.pairs), custom_call_target="tpu_custom_call" | custom-call | tf_op jit(solution)/shard_map/pallas_call | solution.py:370
  44.5 21.2 %all_to_all.11.tendency = bf16[8,16,16,128]{3,2,1,0:T(8,128)(2,1)S(1)} all-to-all(bf16[8,16,16,128]{3,2,1,0:T(8,128)(2,1)S(1)} %shard_map.77), channel_id=1, replica_groups=mesh['sec'=8,'space'=64] {'sec'}, dimensions={0} | all-to-all | bytes 1048576 | tf_op jit(solution)/shard_map/all_to_all | solution.py:375
  65.7 1.5 %shard_map.78 = f32[8,4,64,128]{3,2,1,0:T(8,128)} custom-call(f32[4,64,8,128]{3,2,1,0:T(8,128)S(1)} %get-tuple-element.25.field, bf16[8,16,16,128]{3,2,1,0:T(8,128)(2,1)S(1)} %all_to_all.11.tendency), custom_call_target="tpu_custom_call" | custom-call | tf_op jit(solution)/shard_map/pallas_call | solution.py:376
  (9 shorter events, 0.0 us)
Async XLA Ops:
  0.1 1.2 %copy-start = (f32[8,4,64,128]{3,2,1,0:T(8,128)S(1)}, f32[8,4,64,128]{3,2,1,0:T(8,128)}, u32[]{:S(2)}) copy-start(f32[8,4,64,128]{3,2,1,0:T(8,128)} %density.3) | copy-start | bytes 3145732
  1.3 0.9 %copy-start.2 = (f32[4,64,128]{2,1,0:T(8,128)S(1)}, f32[4,64,128]{2,1,0:T(8,128)}, u32[]{:S(2)}) copy-start(f32[4,64,128]{2,1,0:T(8,128)} %wind.7) | copy-start | bytes 393220
  2.2 3.0 %copy-start.1 = (f32[8,4,64,128]{3,2,1,0:T(8,128)S(1)}, f32[8,4,64,128]{3,2,1,0:T(8,128)}, u32[]{:S(2)}) copy-start(f32[8,4,64,128]{3,2,1,0:T(8,128)} %density.3) | copy-start | bytes 3145732
  2.2 3.0 %copy-start.3 = (f32[4,64,128]{2,1,0:T(8,128)S(1)}, f32[4,64,128]{2,1,0:T(8,128)}, u32[]{:S(2)}) copy-start(f32[4,64,128]{2,1,0:T(8,128)} %wind.7) | copy-start | bytes 393220
  2.2 9.4 %copy-start.4 = (f32[64,64]{1,0:T(8,128)S(1)}, f32[64,64]{1,0:T(8,128)}, u32[]{:S(2)}) copy-start(f32[64,64]{1,0:T(8,128)} %kernel.1) | copy-start | bytes 49156
  2.2 9.4 %copy-start.5 = (s32[64,64]{1,0:T(8,128)S(1)}, s32[64,64]{1,0:T(8,128)}, u32[]{:S(2)}) copy-start(s32[64,64]{1,0:T(8,128)} %target.1) | copy-start | bytes 49156
  2.2 9.4 %copy-start.6 = (bf16[64,64]{1,0:T(8,128)(2,1)S(1)}, bf16[64,64]{1,0:T(8,128)(2,1)}, u32[]{:S(2)}) copy-start(bf16[64,64]{1,0:T(8,128)(2,1)} %breakup.1) | copy-start | bytes 24580
  2.2 9.4 %copy-start.7 = (f32[8]{0:T(128)S(1)}, f32[8]{0:T(128)}, u32[]{:S(2)}) copy-start(f32[8]{0:T(128)} %settling.1) | copy-start | bytes 100
  2.2 9.4 %copy-start.8 = (f32[8]{0:T(128)S(1)}, f32[8]{0:T(128)}, u32[]{:S(2)}) copy-start(f32[8]{0:T(128)} %diffusion.1) | copy-start | bytes 100
  3.2 11.6 %collective-permute-start.1 = (bf16[68,16,128]{2,1,0:T(8,128)(2,1)S(1)}, bf16[68,16,128]{2,1,0:T(8,128)(2,1)S(1)}, u32[]{:S(2)}, u32[]{:S(2)}) collective-permute-start(bf16[68,16,128]{2,1,0:T(8,128)(2,1)S(1)} %get-tuple-element.18), channel_id=1, source_target_pairs={{1,2},{2,1},{3,4},{4,3},{5,6},{6,5},{7,8},{8,7},{9,10},{10,9},{11,... | collective-permute-start | bytes 835592 | tf_op jit(solution)/shard_map/ppermute | solution.py:342
  6.2 8.7 %collective-permute-start = (bf16[68,16,128]{2,1,0:T(8,128)(2,1)S(1)}, bf16[68,16,128]{2,1,0:T(8,128)(2,1)S(1)}, u32[]{:S(2)}, u32[]{:S(2)}) collective-permute-start(bf16[68,16,128]{2,1,0:T(8,128)(2,1)S(1)} %get-tuple-element.17), channel_id=1, source_target_pairs={{0,1},{1,0},{2,3},{3,2},{4,5},{5,4},{6,7},{7,6},{8,9},{9,8},{10,11... | collective-permute-start | bytes 835592 | tf_op jit(solution)/shard_map/ppermute | solution.py:344

commit v3 on v2

v3 whole, which is shorter than its diff:
```python
import functools

import jax
import jax.numpy as jnp
from jax import lax
from jax.experimental import pallas as pl
from jax.experimental.pallas import tpu as pltpu
from jax.sharding import PartitionSpec as P

BF = jnp.bfloat16
F32 = jnp.float32
S = 64
OWN = 8
LAYERS = 4
NY = 64
NZ = 128
HALF = 32
PAIRS = HALF // 2
STEP = 0.25
BLOCKS = 36
DEPTH = BLOCKS * S + 2 * S
LIMIT = 48 * 1024 * 1024


def call(body, out_shape, scratch=(), **specs):
    return pl.pallas_call(
        body,
        out_shape=out_shape,
        scratch_shapes=scratch,
        compiler_params=pltpu.CompilerParams(vmem_limit_bytes=LIMIT),
        **specs,
    )


def oddness():
    return lax.rem(lax.axis_index("space"), 2)


def bring_layer(loaded, out, x):
    zero = jnp.zeros((1, OWN, NZ), F32)
    out[x, 0:1] = zero
    out[x, NY + 1 : NY + 2] = zero

    def rows(p, _):
        for r in range(8):
            out[x, 8 * p + r + 1] = loaded[pl.ds(8 * p + r, OWN, stride=NY), :]
        return 0

    lax.fori_loop(0, NY // 8, rows, 0, unroll=True)


def pack_layer(layer, x, out, at):
    def rows(p, _):
        for r in range(4):
            two = layer[x, pl.ds(8 * p + 2 * r + 1, 2)].reshape(16, NZ)
            out[at + 4 * p + r] = two.astype(BF)
        return 0

    lax.fori_loop(0, NY // 8, rows, 0, unroll=True)


def pack_body(density, wind, out, old, loaded, sems):
    base = 2 - 2 * oddness()
    copies = [
        pltpu.make_async_copy(density.at[:, base + l], loaded.at[l], sems.at[l]) for l in range(2)
    ]
    for copy in copies:
        copy.start()
    for t in range(NY // 16):
        out[2 * HALF + t] = wind[0, 16 * t : 16 * t + 16, :]
    for l in range(2):
        copies[l].wait()
        bring_layer(loaded.at[l].reshape(OWN * NY, NZ), old, l)
        pack_layer(old, l, out, l * HALF)


def block_pairs():
    for g in range(5):
        for q in range(4 if g == 4 else 8):
            yield g, 8 * g + q, (36 + q if g == 4 else (64 - 8 * g + q) % S)


def table_body(kernel, target, breakup, table, rows):
    lane = lax.broadcasted_iota(jnp.int32, (S, NZ), 1)
    second = lane >= S
    column = jnp.where(second, lane - S, lane)

    def blocks(a):
        parts = [a[0:8]]
        for g in range(1, 5):
            count = 4 if g == 4 else 8
            other = 36 if g == 4 else 8 * (8 - g)
            moved = pltpu.roll(a, S + 8 * g, 1)[other : other + count]
            own = a[8 * g : 8 * g + count]
            parts.append(jnp.where(column[0:count] >= 8 * g, own, moved))
        return parts

    def store(at, a):
        for g, part in enumerate(blocks(a)):
            rows[at, 8 * g : 8 * g + part.shape[0], :] = part

    def twice(a):
        return jnp.concatenate([a, a], 1)

    rates = kernel[...].astype(BF).astype(F32)
    targets = target[...].astype(F32)
    j = blocks(column.astype(F32))
    i = blocks(lax.broadcasted_iota(jnp.int32, (S, NZ), 0).astype(F32))
    store(0, twice(targets))
    store(1, twice(jnp.transpose(targets)))
    for g, (one, two) in enumerate(zip(blocks(twice(rates)), blocks(twice(jnp.transpose(rates))))):
        rows[2, 8 * g : 8 * g + one.shape[0], :] = jnp.where(j[g] >= i[g], one, 0.0)
        rows[3, 8 * g : 8 * g + one.shape[0], :] = jnp.where(j[g] > i[g], two, 0.0)
    k = lax.broadcasted_iota(jnp.int32, (S, NZ), 0).astype(F32)
    for t in range(BLOCKS // 2):
        to, to_t, rate, rate_t = [
            jnp.where(second[0:1], rows[q, 2 * t + 1 : 2 * t + 2, :], rows[q, 2 * t : 2 * t + 1, :])
            for q in range(4)
        ]
        one = jnp.where(to == k, rate, 0.0) + jnp.where(to_t == k, rate_t, 0.0)
        table[0:S, t * NZ : (t + 1) * NZ] = one.astype(BF)
    table[S:, : BLOCKS * S] = jnp.zeros((S, BLOCKS * S), BF)
    none = jnp.zeros((S, S), F32)
    table[0:S, BLOCKS * S :] = jnp.concatenate([breakup[...].astype(F32), none], 1).astype(BF)
    table[S:, BLOCKS * S :] = jnp.concatenate([rates, none], 1).astype(BF)


def spread_rows(rows):
    return jnp.broadcast_to(rows[:, None, :], (8, OWN, NZ))


def within(ten, u, constants):
    here, from_above, from_below, spread = constants
    c = ten[1:9]
    return (
        c * (here - jnp.abs(u))
        + pltpu.roll(c, NZ - 1, 2) * from_above
        + pltpu.roll(c, 1, 2) * from_below
        + (ten[0:8] + ten[2:10]) * spread
    )


def from_west_of(u, spread):
    return spread + jnp.maximum(u, 0.0)


def from_east_of(u, spread):
    return spread - jnp.minimum(u, 0.0)


def per_section(ref):
    row = lax.broadcasted_iota(jnp.int32, (OWN, OWN), 0)
    column = lax.broadcasted_iota(jnp.int32, (OWN, OWN), 1)
    spread = jnp.where(row == column, jnp.broadcast_to(ref[...], (OWN, OWN)), 0.0)
    return jnp.broadcast_to(jnp.sum(spread, axis=1, keepdims=True), (OWN, NZ))


def inner_body(
    settling, diffusion, density, kept, wind, kernel, target, breakup,
    old, field, reach, constants, table, mid, rows,
):
    table_body(kernel, target, breakup, table, rows)
    sink, spread = per_section(settling), per_section(diffusion)
    lane = lax.broadcasted_iota(jnp.int32, (OWN, NZ), 1)
    held = (
        1.0 - sink - 6.0 * spread,
        jnp.where(lane == NZ - 1, 0.0, sink + spread),
        jnp.where(lane == 0, 0.0, spread),
        spread,
    )
    for i in range(4):
        constants[i] = held[i]
    zero = jnp.zeros((1, OWN, NZ), F32)
    for x in range(LAYERS):
        mid[x, 0:1] = zero
        mid[x, NY + 1 : NY + 2] = zero

    rest = 2 * oddness()
    own = 2 - rest
    for l in range(2):
        old[own + l] = kept[l]
        for y in (0, NY + 1):
            old[rest + l, y : y + 1] = zero
        start = (rest + l) * NY
        for y in range(NY):
            old[rest + l, y + 1] = density[pl.ds(start + y, OWN, stride=LAYERS * NY), :]

    def substep(ref, y, store, store_reach=None):
        for x in range(LAYERS):
            u = spread_rows(wind[x, pl.ds(y, 8), :])
            west, east = from_west_of(u, spread), from_east_of(u, spread)
            value = within(ref[x, pl.ds(y, 10)], u, held)
            if x > 0:
                value = value + ref[x - 1, pl.ds(y + 1, 8)] * west
            if x < LAYERS - 1:
                value = value + ref[x + 1, pl.ds(y + 1, 8)] * east
            store(x, value)
            if store_reach is not None:
                store_reach(x, west if x < 2 else east)

    def first(b, _):
        y = pl.multiple_of(8 * b, 8)

        def store(x, value):
            mid[x, pl.ds(y + 1, 8)] = value

        def store_reach(x, value):
            reach[x, pl.ds(y, 8)] = value

        substep(old, y, store, store_reach)
        return 0

    def second(b, _):
        y = pl.multiple_of(8 * b, 8)

        def store(x, value):
            field[x, pl.ds(y, 8)] = value

        substep(mid, y, store)
        return 0

    lax.fori_loop(0, NY // 8, first, 0, unroll=True)
    lax.fori_loop(0, NY // 8, second, 0, unroll=True)


def side_body(
    plain, slabs, message, wind, old, inner, reach, constants, *refs
):
    if plain:
        done, field, rounded, halo, change, beyond, raw = refs
    else:
        field, rounded, halo, change, beyond = refs
    odd = oddness()
    side = odd if plain else 1 - odd
    edge = 3 * side
    next_layer = 1 + side
    sign = 1.0 - 2.0 * side.astype(F32)
    inside = (lax.axis_index("space") != side * (slabs - 1)).astype(F32)
    held = tuple(constants[i] for i in range(4))
    spread = held[3]
    zero = jnp.zeros((1, OWN, NZ), F32)
    for ref in (halo, change):
        ref[0:1] = zero
        ref[NY + 1 : NY + 2] = zero
    if plain:
        for t in range(LAYERS):
            rounded[t] = done[t]
        for s in range(OWN):
            for l in range(2):
                raw[l, s * NY : (s + 1) * NY, :] = message[2 * s + l].astype(F32)
        for y in range(NY):
            halo[y + 1] = raw[1 - side, pl.ds(y, OWN, stride=NY), :]
    else:
        for p in range(HALF):
            two = message[(1 - side) * HALF + p].astype(F32).reshape(2, OWN, NZ)
            halo[2 * p + 1 : 2 * p + 3] = two

    for b in range(NY // 8):
        y = 8 * b
        if plain:
            far = [raw[side, pl.ds(y + r, OWN, stride=NY), :][None] for r in range(8)]
            winds = message[2 * OWN + 1 - side, 16 * (b // 2) : 16 * (b // 2) + 16, :].astype(F32)
        else:
            far = [
                message[side * HALF + 4 * b + h].astype(F32).reshape(2, OWN, NZ) for h in range(4)
            ]
            winds = message[2 * HALF + b // 2].astype(F32)
        far = jnp.concatenate(far, 0)
        u = spread_rows(winds[8 * (b % 2) : 8 * (b % 2) + 8])
        outward = sign * u
        ten = halo[y : y + 10]
        value = (
            within(ten, u, held)
            + far * (spread + jnp.maximum(outward, 0.0))
            + old[edge, y + 1 : y + 9] * (spread - jnp.minimum(outward, 0.0))
        )
        beyond[y : y + 8] = value * inside
        change[y + 1 : y + 9] = ten[1:9] * reach[edge, y : y + 8]

    for b in range(NY // 8):
        y = 8 * b
        u = spread_rows(wind[edge, y : y + 8, :])
        ten = change[y : y + 10]
        outer = inner[edge, y : y + 8] + within(ten, u, held)
        outer = outer + beyond[y : y + 8] * reach[edge, y : y + 8]
        second = inner[next_layer, y : y + 8] + ten[1:9] * reach[next_layer, y : y + 8]
        for at, value in ((side, outer), (1 - side, second)):
            field[at, y : y + 8] = value
            for h in range(4):
                two = value[2 * h : 2 * h + 2].reshape(16, NZ)
                p = 4 * b + h
                slot = (LAYERS if plain else 0) + 2 * at + p // PAIRS
                rounded[slot, p % PAIRS] = two.astype(BF)


WIDE = 16


def kinetics_body(cells, table, out, wide, products):
    products[DEPTH - S :, :] = jnp.zeros((S, 2 * NZ * WIDE), BF)

    def step(q, _):
        parts = []
        for u in range(WIDE):
            x = cells[:, WIDE * q + u].astype(F32)
            parts += [x[:, 0:8, :].reshape(S, NZ), x[:, 8:16, :].reshape(S, NZ)]
        n = jnp.concatenate(parts, 1)
        wide[...] = n
        for b, (g, i, other) in enumerate(block_pairs()):
            n_i, n_other = wide[i : i + 1, :], wide[other : other + 1, :]
            rows = []
            for t in range(8):
                if t < g:
                    at = 8 * (t + 8 - g)
                    rows.append(n[at : at + 8] * n_other)
                else:
                    rows.append(n[8 * t : 8 * t + 8] * n_i)
            products[S * b : S * (b + 1), :] = jnp.concatenate(rows, 0).astype(BF)
        products[BLOCKS * S : BLOCKS * S + S, :] = n.astype(BF)
        sums = jnp.dot(table[...], products[...], preferred_element_type=F32)
        total = sums[0:S] - n * sums[S:]
        for u in range(WIDE):
            at = 2 * NZ * u
            a = total[:, at : at + NZ].reshape(8, OWN, NZ)
            b = total[:, at + NZ : at + 2 * NZ].reshape(8, OWN, NZ)
            out[:, WIDE * q + u] = jnp.concatenate([a, b], 1).astype(BF)
        return 0

    lax.fori_loop(0, PAIRS // WIDE, step, 0)


def finish_body(near, far, tendency, out, held, sems):
    odd = oddness()
    copies = []
    for x in range(LAYERS):
        layer = held.at[x].reshape(OWN * NY, NZ)
        field, at = (near, x) if x < 2 else (far, x - 2)

        def rows(p, _):
            for half in range(2):
                y = half * HALF + 2 * p
                two = STEP * tendency[2 * x + half, p].astype(F32)
                layer[pl.ds(y, OWN, stride=NY), :] = field[at, y] + two[0:8]
                layer[pl.ds(y + 1, OWN, stride=NY), :] = field[at, y + 1] + two[8:16]
            return 0

        lax.fori_loop(0, PAIRS, rows, 0, unroll=True)
        place = at + 2 * (1 - odd) if x < 2 else at + 2 * odd
        copies.append(pltpu.make_async_copy(held.at[x], out.at[:, place], sems.at[x]))
        copies[x].start()
    for copy in copies:
        copy.wait()


def per_device(density, wind_speed, settling, diffusion, breakup, coag_kernel, pair_target):
    slabs = lax.axis_size("space")
    odd = oddness()
    vmem = pl.BlockSpec(memory_space=pltpu.VMEM)
    hbm = pl.BlockSpec(memory_space=pltpu.HBM)
    message = jax.ShapeDtypeStruct((2 * HALF + NY // 16, 16, NZ), BF)
    block = jax.ShapeDtypeStruct((8, PAIRS, 16, NZ), BF)
    cells_f32 = jax.ShapeDtypeStruct((LAYERS, NY, OWN, NZ), F32)
    padded = (LAYERS, NY + 2, OWN, NZ)

    both = jnp.concatenate([density, wind_speed[None]], 0)
    to_other = lax.dynamic_slice_in_dim(both, 2 * odd, 2, 1).astype(BF).reshape(2 * OWN + 2, NY, NZ)
    other = lax.ppermute(to_other, "space", [(i, ((i + 1) ^ 1) - 1) for i in range(1, slabs - 1)])
    wind_held = lax.optimization_barrier(wind_speed)
    to_partner, kept = call(
        pack_body,
        (message, jax.ShapeDtypeStruct((2, NY + 2, OWN, NZ), F32)),
        scratch=(
            pltpu.VMEM((2, OWN, NY, NZ), F32),
            pltpu.SemaphoreType.DMA((2,)),
        ),
        in_specs=[hbm, vmem],
    )(density, jnp.where(odd == 0, wind_held[LAYERS - 1 :], wind_held[0:1]).astype(BF))
    partner = lax.ppermute(to_partner, "space", [(i, i ^ 1) for i in range(slabs)])
    old, inner, reach, constants, table = call(
        inner_body,
        (
            jax.ShapeDtypeStruct(padded, F32),
            cells_f32,
            cells_f32,
            jax.ShapeDtypeStruct((4, OWN, NZ), F32),
            jax.ShapeDtypeStruct((2 * S, DEPTH), BF),
        ),
        scratch=(pltpu.VMEM(padded, F32), pltpu.VMEM((4, BLOCKS, NZ), F32)),
    )(
        settling.reshape(1, OWN), diffusion.reshape(1, OWN), density.reshape(OWN * LAYERS * NY, NZ), kept, wind_speed,
        coag_kernel, pair_target, breakup,
    )
    half = jax.ShapeDtypeStruct((2, NY, OWN, NZ), F32)
    half_block = jax.ShapeDtypeStruct((4, PAIRS, 16, NZ), BF)
    row_block = (NY + 2, OWN, NZ)
    scratch = (pltpu.VMEM(row_block, F32), pltpu.VMEM(row_block, F32), pltpu.VMEM((NY, OWN, NZ), F32))
    rest = (wind_speed, old, inner, reach, constants)
    near, near_rounded = call(
        functools.partial(side_body, False, slabs),
        (half, half_block),
        scratch=scratch,
    )(partner, *rest)
    far, rounded = call(
        functools.partial(side_body, True, slabs),
        (half, block),
        scratch=scratch + (pltpu.VMEM((2, OWN * NY, NZ), F32),),
    )(other, *rest, near_rounded)
    cells = lax.all_to_all(rounded, "sec", split_axis=0, concat_axis=0, tiled=True)
    width = 2 * NZ * WIDE
    tendency = call(
        kinetics_body,
        block,
        scratch=(pltpu.VMEM((S, width), F32), pltpu.VMEM((DEPTH, width), BF)),
    )(cells, table)
    returned = lax.all_to_all(tendency, "sec", split_axis=0, concat_axis=0, tiled=True)
    return call(
        finish_body,
        jax.ShapeDtypeStruct((OWN, LAYERS, NY, NZ), F32),
        scratch=(pltpu.VMEM((LAYERS, OWN, NY, NZ), F32), pltpu.SemaphoreType.DMA((LAYERS,))),
        in_specs=[vmem, vmem, vmem],
        out_specs=hbm,
    )(near, far, returned)


def solution(mesh):
    in_specs = (
        P("sec", "space", None, None),
        P("space", None, None),
        P("sec"),
        P("sec"),
        P(),
        P(),
        P(),
    )
    out_specs = P("sec", "space", None, None)
    return jax.shard_map(
        per_device, mesh=mesh, in_specs=in_specs, out_specs=out_specs, check_vma=False
    )
```

time: 67.5 us -> 62.7 us (0.929)
  Pallas kernels: 12.5 us -> 8.4 us
  local copies, waits for them, and re-layouts: 2.16 us -> 0.03 us
  other arithmetic: 0.23 us -> 1.19 us
  waiting for transfers between devices: 0.01 us -> 0.89 us
    unnamed x18 -> x14, local copies, waits for them, and re-layouts: 2.16 us -> 0.03 us
    pallas_call x3, Pallas kernels: 3.46 us -> 1.56 us  [the longest x1 0.71 us: per_device(): call(functools.partial(side_body, True, slabs), (half, block), scratch=sc...]
    convert_element_type x0 -> x2, other arithmetic: none -> 1.19 us  [the longest x1 1.18 us: per_device(): lax.dynamic_slice_in_dim(both, 2 * odd, 2, 1).astype(BF)]
    pallas_call x1, Pallas kernels: 3.26 us -> 2.16 us  [per_device(): call(inner_body, (jax.ShapeDtypeStruct(padded, F32), cells_f32, cells_f32...]
    pallas_call x1, Pallas kernels: 4.22 us -> 3.22 us  [per_device(): call(kinetics_body, block, scratch=(pltpu.VMEM((S, width), F32), pltpu.VM...]
    ppermute x1, waiting for transfers between devices: 0.01 us -> 0.89 us  [per_device(): lax.ppermute(to_other, 'space', [(i, (i + 1 ^ 1) - 1) for i in range(1, s...]
  transfers between devices with their start and end apart: 2 -> 2, of which waited for: 0 -> 1; matrix products, arithmetic and copies ran while one was open for 0% -> 0% of each run, Pallas kernels for 6% -> 5%
where the time goes in v3:
time: 62.7 us; the launch traced here: 62.5 us
  blocking collectives  44.6 us (71%)
  Pallas kernels  8.4 us (13%)
  starting transfers between devices  7.17 us (11%)
  other arithmetic  1.19 us (2%)
  waiting for transfers between devices  0.89 us (1%)
    all_to_all x1, blocking collectives, per_device(): lax.all_to_all(rounded, 'sec', split_axis=0, concat_axis=0, tiled=True)  23.4 us
    all_to_all x1, blocking collectives, per_device(): lax.all_to_all(tendency, 'sec', split_axis=0, concat_axis=0, tiled=True)  21.2 us
    ppermute x1, starting transfers between devices, per_device(): lax.ppermute(to_partner, 'space', [(i, i ^ 1) for i in range(slabs)])  5.25 us
    pallas_call x1, Pallas kernels, per_device(): call(kinetics_body, block, scratch=(pltpu.VMEM((S, width), F32), pltpu.VM...  3.22 us
    pallas_call x1, Pallas kernels, per_device(): call(inner_body, (jax.ShapeDtypeStruct(padded, F32), cells_f32, cells_f32...  2.16 us
    ppermute x1, starting transfers between devices, per_device(): lax.ppermute(to_other, 'space', [(i, (i + 1 ^ 1) - 1) for i in range(1, s...  1.92 us
    pallas_call x1, Pallas kernels, per_device(): call(finish_body, jax.ShapeDtypeStruct((OWN, LAYERS, NY, NZ), F32), scrat...  1.47 us
  transfers between devices with their start and end apart: 2, of which 1 were waited for; matrix products, arithmetic and copies ran while one was open for 0% of the time, Pallas kernels for 5%

profile of v3, /device:TPU:216, one launch (start us, length us, event | category | flops | bytes accessed | tf_op | source)
XLA Modules:
  0.0 62.5 jit_solution(9048669349042699519)
XLA Ops:
  0.0 0.0 copy-start.3
  0.0 0.0 copy-start.4
  0.0 0.0 copy-start.5
  0.0 0.0 copy-start.6
  0.0 1.2 %fusion.1 = bf16[9,2,64,128]{3,2,1,0:T(8,128)(2,1)S(1)} fusion(s32[]{:T(128)S(6)} %select_n.13, f32[8,4,64,128]{3,2,1,0:T(8,128)} %density.1, f32[1,4,64,128]{3,2,1,0:T(8,128)} %bitcast.6), kind=kLoop, calls=%fused_computation.3 | loop fusion | flops 147456 | bytes 1474564 | tf_op jit(solution)/shard_map/convert_element_type | solution.py:366
  1.2 1.9 %collective-permute-start.1 = (bf16[18,64,128]{2,1,0:T(8,128)(2,1)S(1)}, bf16[18,64,128]{2,1,0:T(8,128)(2,1)S(1)}, u32[]{:S(2)}, u32[]{:S(2)}) collective-permute-start(bf16[18,64,128]{2,1,0:T(8,128)(2,1)S(1)} %bitcast.9), channel_id=1, source_target_pairs={{1,2},{2,1},{3,4},{4,3},{5,6},{6,5},{7,8},{8,7},{9,10},{10,9},{11,... | collective-permute-start | bytes 884744 | tf_op jit(solution)/shard_map/ppermute | solution.py:367
  3.2 0.0 copy-done.1
  3.2 0.0 copy-done
  3.2 0.4 shard_map.73
  3.6 5.3 %collective-permute-start = (bf16[68,16,128]{2,1,0:T(8,128)(2,1)S(1)}, bf16[68,16,128]{2,1,0:T(8,128)(2,1)S(1)}, u32[]{:S(2)}, u32[]{:S(2)}) collective-permute-start(bf16[68,16,128]{2,1,0:T(8,128)(2,1)S(1)} %get-tuple-element.16), channel_id=1, source_target_pairs={{0,1},{1,0},{2,3},{3,2},{4,5},{5,4},{6,7},{7,6},{8,9},{9,8},{10,11... | collective-permute-start | bytes 835592 | tf_op jit(solution)/shard_map/ppermute | solution.py:378
  8.9 0.0 copy-done.2
  8.9 0.0 copy-done.3
  8.9 0.0 copy-done.4
  8.9 0.0 copy-done.5
  8.9 0.0 copy-done.6
  8.9 2.2 %shard_map.74 = (f32[4,66,8,128]{3,2,1,0:T(8,128)S(1)}, f32[4,64,8,128]{3,2,1,0:T(8,128)S(1)}, f32[4,64,8,128]{3,2,1,0:T(8,128)S(1)}, f32[4,8,128]{2,1,0:T(8,128)S(1)}, bf16[128,2432]{1,0:T(8,128)(2,1)S(1)}) custom-call(f32[1,8]{1,0:T(1,128)S(1)} %bitcast.7, f32[1,8]{1,0:T(1,128)S(1)} %bitcast.8, f32[2048,128]{1,0:T(8,128)S(1)} %bitcast.5, ...), custom_call_target="tpu_custom_call" | custom-call | tf_op jit(solution)/shard_map/pallas_call | solution.py:379
  11.1 0.0 collective-permute-done.message
  11.1 0.5 shard_map.75
  11.6 0.9 %collective-permute-done.1.message = bf16[18,64,128]{2,1,0:T(8,128)(2,1)S(1)} collective-permute-done((bf16[18,64,128]{2,1,0:T(8,128)(2,1)S(1)}, bf16[18,64,128]{2,1,0:T(8,128)(2,1)S(1)}, u32[]{:S(2)}, u32[]{:S(2)}) %collective-permute-start.1) | collective-permute-done | bytes 294944 | tf_op jit(solution)/shard_map/ppermute | solution.py:367
  12.4 0.7 %shard_map.76 = (f32[2,64,8,128]{3,2,1,0:T(8,128)S(1)}, bf16[8,16,16,128]{3,2,1,0:T(8,128)(2,1)S(1)}) custom-call(bf16[18,64,128]{2,1,0:T(8,128)(2,1)S(1)} %collective-permute-done.1.message, f32[4,64,128]{2,1,0:T(8,128)S(1)} %copy-done.1, f32[4,66,8,128]{3,2,1,0:T(8,128)S(1)} %get-tuple-element.18.old, f32[4,64,8,128]{3,2,1,0:T(8,128)S(1)} %get-tuple-element.19.inner, ...), custom_call_target="tpu_custom_call" | custom-call | tf_op jit(solution)/shard_map/pallas_call | solution.py:403
  13.2 23.4 %all_to_all.10.cells = bf16[8,16,16,128]{3,2,1,0:T(8,128)(2,1)S(1)} all-to-all(bf16[8,16,16,128]{3,2,1,0:T(8,128)(2,1)S(1)} %get-tuple-element.25), channel_id=1, replica_groups=mesh['sec'=8,'space'=64] {'sec'}, dimensions={0} | all-to-all | bytes 1048576 | tf_op jit(solution)/shard_map/all_to_all | solution.py:408
  36.6 3.2 %shard_map.77 = bf16[8,16,16,128]{3,2,1,0:T(8,128)(2,1)S(1)} custom-call(bf16[8,16,16,128]{3,2,1,0:T(8,128)(2,1)S(1)} %all_to_all.10.cells, bf16[128,2432]{1,0:T(8,128)(2,1)S(1)} %get-tuple-element.26.table), custom_call_target="tpu_custom_call" | custom-call | tf_op jit(solution)/shard_map/pallas_call | solution.py:410
  39.8 21.2 %all_to_all.11.tendency = bf16[8,16,16,128]{3,2,1,0:T(8,128)(2,1)S(1)} all-to-all(bf16[8,16,16,128]{3,2,1,0:T(8,128)(2,1)S(1)} %shard_map.77), channel_id=1, replica_groups=mesh['sec'=8,'space'=64] {'sec'}, dimensions={0} | all-to-all | bytes 1048576 | tf_op jit(solution)/shard_map/all_to_all | solution.py:415
  61.0 1.5 %shard_map.78 = f32[8,4,64,128]{3,2,1,0:T(8,128)} custom-call(f32[2,64,8,128]{3,2,1,0:T(8,128)S(1)} %get-tuple-element.22.near, f32[2,64,8,128]{3,2,1,0:T(8,128)S(1)} %get-tuple-element.24.far, bf16[8,16,16,128]{3,2,1,0:T(8,128)(2,1)S(1)} %all_to_all.11.tendency), custom_call_target="tpu_custom_call" | custom-call | tf_op jit(solution)/shard_map/pallas_call | solution.py:416
  (4 shorter events, 0.0 us)
Async XLA Ops:
  0.0 3.2 %copy-start = (f32[8,4,64,128]{3,2,1,0:T(8,128)S(1)}, f32[8,4,64,128]{3,2,1,0:T(8,128)}, u32[]{:S(2)}) copy-start(f32[8,4,64,128]{3,2,1,0:T(8,128)} %density.1) | copy-start | bytes 3145732
  0.0 3.2 %copy-start.1 = (f32[4,64,128]{2,1,0:T(8,128)S(1)}, f32[4,64,128]{2,1,0:T(8,128)}, u32[]{:S(2)}) copy-start(f32[4,64,128]{2,1,0:T(8,128)} %wind.5) | copy-start | bytes 393220
  0.0 8.9 %copy-start.2 = (f32[64,64]{1,0:T(8,128)S(1)}, f32[64,64]{1,0:T(8,128)}, u32[]{:S(2)}) copy-start(f32[64,64]{1,0:T(8,128)} %kernel.1) | copy-start | bytes 49156
  0.0 8.9 %copy-start.3 = (s32[64,64]{1,0:T(8,128)S(1)}, s32[64,64]{1,0:T(8,128)}, u32[]{:S(2)}) copy-start(s32[64,64]{1,0:T(8,128)} %target.1) | copy-start | bytes 49156
  0.0 8.9 %copy-start.4 = (bf16[64,64]{1,0:T(8,128)(2,1)S(1)}, bf16[64,64]{1,0:T(8,128)(2,1)}, u32[]{:S(2)}) copy-start(bf16[64,64]{1,0:T(8,128)(2,1)} %breakup.1) | copy-start | bytes 24580
  0.0 8.9 %copy-start.5 = (f32[8]{0:T(128)S(1)}, f32[8]{0:T(128)}, u32[]{:S(2)}) copy-start(f32[8]{0:T(128)} %param.9) | copy-start | bytes 100
  0.0 8.9 %copy-start.6 = (f32[8]{0:T(128)S(1)}, f32[8]{0:T(128)}, u32[]{:S(2)}) copy-start(f32[8]{0:T(128)} %param.10) | copy-start | bytes 100
  1.2 11.2 %collective-permute-start.1 = (bf16[18,64,128]{2,1,0:T(8,128)(2,1)S(1)}, bf16[18,64,128]{2,1,0:T(8,128)(2,1)S(1)}, u32[]{:S(2)}, u32[]{:S(2)}) collective-permute-start(bf16[18,64,128]{2,1,0:T(8,128)(2,1)S(1)} %bitcast.9), channel_id=1, source_target_pairs={{1,2},{2,1},{3,4},{4,3},{5,6},{6,5},{7,8},{8,7},{9,10},{10,9},{11,... | collective-permute-start | bytes 884744 | tf_op jit(solution)/shard_map/ppermute | solution.py:367
  3.6 7.5 %collective-permute-start = (bf16[68,16,128]{2,1,0:T(8,128)(2,1)S(1)}, bf16[68,16,128]{2,1,0:T(8,128)(2,1)S(1)}, u32[]{:S(2)}, u32[]{:S(2)}) collective-permute-start(bf16[68,16,128]{2,1,0:T(8,128)(2,1)S(1)} %get-tuple-element.16), channel_id=1, source_target_pairs={{0,1},{1,0},{2,3},{3,2},{4,5},{5,4},{6,7},{7,6},{8,9},{9,8},{10,11... | collective-permute-start | bytes 835592 | tf_op jit(solution)/shard_map/ppermute | solution.py:378

commit v4 on v3

--- a/solution.py
+++ b/solution.py
@@ -36,17 +36,16 @@
     return lax.rem(lax.axis_index("space"), 2)
 
 
+def swapped(block):
+    return jnp.swapaxes(block, 0, 1)
+
+
 def bring_layer(loaded, out, x):
     zero = jnp.zeros((1, OWN, NZ), F32)
     out[x, 0:1] = zero
     out[x, NY + 1 : NY + 2] = zero
-
-    def rows(p, _):
-        for r in range(8):
-            out[x, 8 * p + r + 1] = loaded[pl.ds(8 * p + r, OWN, stride=NY), :]
-        return 0
-
-    lax.fori_loop(0, NY // 8, rows, 0, unroll=True)
+    for y in range(0, NY, 8):
+        out[x, y + 1 : y + 9] = swapped(loaded[:, y : y + 8, :])
 
 
 def pack_layer(layer, x, out, at):
@@ -70,7 +69,7 @@
         out[2 * HALF + t] = wind[0, 16 * t : 16 * t + 16, :]
     for l in range(2):
         copies[l].wait()
-        bring_layer(loaded.at[l].reshape(OWN * NY, NZ), old, l)
+        bring_layer(loaded.at[l], old, l)
         pack_layer(old, l, out, l * HALF)
 
 
@@ -179,11 +178,7 @@
     own = 2 - rest
     for l in range(2):
         old[own + l] = kept[l]
-        for y in (0, NY + 1):
-            old[rest + l, y : y + 1] = zero
-        start = (rest + l) * NY
-        for y in range(NY):
-            old[rest + l, y + 1] = density[pl.ds(start + y, OWN, stride=LAYERS * NY), :]
+        bring_layer(density.at[:, rest + l], old, rest + l)
 
     def substep(ref, y, store, store_reach=None):
         for x in range(LAYERS):
@@ -227,7 +222,7 @@
     plain, slabs, message, wind, old, inner, reach, constants, *refs
 ):
     if plain:
-        done, field, rounded, halo, change, beyond, raw = refs
+        done, field, rounded, halo, change, beyond, far = refs
     else:
         field, rounded, halo, change, beyond = refs
     odd = oddness()
@@ -245,11 +240,12 @@
     if plain:
         for t in range(LAYERS):
             rounded[t] = done[t]
-        for s in range(OWN):
-            for l in range(2):
-                raw[l, s * NY : (s + 1) * NY, :] = message[2 * s + l].astype(F32)
-        for y in range(NY):
-            halo[y + 1] = raw[1 - side, pl.ds(y, OWN, stride=NY), :]
+        for y in range(0, NY, 16):
+            for l, out, first in ((1 - side, halo, 1), (side, far, 0)):
+                rows = [message[2 * s + l, y : y + 16, :].astype(F32)[None] for s in range(OWN)]
+                rows = jnp.concatenate(rows, 0)
+                out[y + first : y + first + 8] = swapped(rows[:, 0:8])
+                out[y + first + 8 : y + first + 16] = swapped(rows[:, 8:16])
     else:
         for p in range(HALF):
             two = message[(1 - side) * HALF + p].astype(F32).reshape(2, OWN, NZ)
@@ -258,20 +254,20 @@
     for b in range(NY // 8):
         y = 8 * b
         if plain:
-            far = [raw[side, pl.ds(y + r, OWN, stride=NY), :][None] for r in range(8)]
+            farther = far[y : y + 8]
             winds = message[2 * OWN + 1 - side, 16 * (b // 2) : 16 * (b // 2) + 16, :].astype(F32)
         else:
-            far = [
+            farther = [
                 message[side * HALF + 4 * b + h].astype(F32).reshape(2, OWN, NZ) for h in range(4)
             ]
+            farther = jnp.concatenate(farther, 0)
             winds = message[2 * HALF + b // 2].astype(F32)
-        far = jnp.concatenate(far, 0)
         u = spread_rows(winds[8 * (b % 2) : 8 * (b % 2) + 8])
         outward = sign * u
         ten = halo[y : y + 10]
         value = (
             within(ten, u, held)
-            + far * (spread + jnp.maximum(outward, 0.0))
+            + farther * (spread + jnp.maximum(outward, 0.0))
             + old[edge, y + 1 : y + 9] * (spread - jnp.minimum(outward, 0.0))
         )
         beyond[y : y + 8] = value * inside
@@ -332,22 +328,17 @@
 def finish_body(near, far, tendency, out, held, sems):
     odd = oddness()
     copies = []
-    for x in range(LAYERS):
-        layer = held.at[x].reshape(OWN * NY, NZ)
+    for slot in range(2 * LAYERS):
+        x, first = slot // 2, slot % 2 * HALF
         field, at = (near, x) if x < 2 else (far, x - 2)
-
-        def rows(p, _):
-            for half in range(2):
-                y = half * HALF + 2 * p
-                two = STEP * tendency[2 * x + half, p].astype(F32)
-                layer[pl.ds(y, OWN, stride=NY), :] = field[at, y] + two[0:8]
-                layer[pl.ds(y + 1, OWN, stride=NY), :] = field[at, y + 1] + two[8:16]
-            return 0
-
-        lax.fori_loop(0, PAIRS, rows, 0, unroll=True)
         place = at + 2 * (1 - odd) if x < 2 else at + 2 * odd
-        copies.append(pltpu.make_async_copy(held.at[x], out.at[:, place], sems.at[x]))
-        copies[x].start()
+        for y in range(0, HALF, 8):
+            change = [tendency[slot, y // 2 + r].astype(F32).reshape(2, OWN, NZ) for r in range(4)]
+            value = field[at, first + y : first + y + 8] + STEP * jnp.concatenate(change, 0)
+            held[slot, :, y : y + 8, :] = swapped(value)
+        target = out.at[:, place, pl.ds(first, HALF)]
+        copies.append(pltpu.make_async_copy(held.at[slot], target, sems.at[slot]))
+        copies[slot].start()
     for copy in copies:
         copy.wait()
 
@@ -387,7 +378,7 @@
         ),
         scratch=(pltpu.VMEM(padded, F32), pltpu.VMEM((4, BLOCKS, NZ), F32)),
     )(
-        settling.reshape(1, OWN), diffusion.reshape(1, OWN), density.reshape(OWN * LAYERS * NY, NZ), kept, wind_speed,
+        settling.reshape(1, OWN), diffusion.reshape(1, OWN), density, kept, wind_speed,
         coag_kernel, pair_target, breakup,
     )
     half = jax.ShapeDtypeStruct((2, NY, OWN, NZ), F32)
@@ -403,7 +394,7 @@
     far, rounded = call(
         functools.partial(side_body, True, slabs),
         (half, block),
-        scratch=scratch + (pltpu.VMEM((2, OWN * NY, NZ), F32),),
+        scratch=scratch + (pltpu.VMEM((NY, OWN, NZ), F32),),
     )(other, *rest, near_rounded)
     cells = lax.all_to_all(rounded, "sec", split_axis=0, concat_axis=0, tiled=True)
     width = 2 * NZ * WIDE
@@ -416,7 +407,10 @@
     return call(
         finish_body,
         jax.ShapeDtypeStruct((OWN, LAYERS, NY, NZ), F32),
-        scratch=(pltpu.VMEM((LAYERS, OWN, NY, NZ), F32), pltpu.SemaphoreType.DMA((LAYERS,))),
+        scratch=(
+            pltpu.VMEM((2 * LAYERS, OWN, HALF, NZ), F32),
+            pltpu.SemaphoreType.DMA((2 * LAYERS,)),
+        ),
         in_specs=[vmem, vmem, vmem],
         out_specs=hbm,
     )(near, far, returned)

time: 62.7 us -> 62.1 us (level)
  Pallas kernels: 8.4 us -> 7.51 us
  transfers between devices with their start and end apart: 2 -> 2, of which waited for: 1 -> 1; matrix products, arithmetic and copies ran while one was open for 0% -> 0% of each run, Pallas kernels for 5% -> 4%
where the time goes in v4:
time: 62.1 us; the launch traced here: 61.9 us
  blocking collectives  44.6 us (72%)
  Pallas kernels  7.51 us (12%)
  starting transfers between devices  7.17 us (12%)
  waiting for transfers between devices  1.2 us (2%)
  other arithmetic  1.19 us (2%)
    all_to_all x1, blocking collectives, per_device(): lax.all_to_all(rounded, 'sec', split_axis=0, concat_axis=0, tiled=True)  23.3 us
    all_to_all x1, blocking collectives, per_device(): lax.all_to_all(tendency, 'sec', split_axis=0, concat_axis=0, tiled=True)  21.3 us
    ppermute x1, starting transfers between devices, per_device(): lax.ppermute(to_partner, 'space', [(i, i ^ 1) for i in range(slabs)])  5.25 us
    pallas_call x1, Pallas kernels, per_device(): call(kinetics_body, block, scratch=(pltpu.VMEM((S, width), F32), pltpu.VM...  3.22 us
    pallas_call x1, Pallas kernels, per_device(): call(inner_body, (jax.ShapeDtypeStruct(padded, F32), cells_f32, cells_f32...  2.06 us
    ppermute x1, starting transfers between devices, per_device(): lax.ppermute(to_other, 'space', [(i, (i + 1 ^ 1) - 1) for i in range(1, s...  1.92 us
  transfers between devices with their start and end apart: 2, of which 1 were waited for; matrix products, arithmetic and copies ran while one was open for 0% of the time, Pallas kernels for 4%

profile of v4, /device:TPU:216, one launch (start us, length us, event | category | flops | bytes accessed | tf_op | source)
XLA Modules:
  0.0 61.9 jit_solution(4680261774573939055)
XLA Ops:
  0.0 0.0 copy-start.3
  0.0 0.0 copy-start.4
  0.0 0.0 copy-start.5
  0.0 0.0 copy-start.6
  0.0 1.2 %fusion.1 = bf16[9,2,64,128]{3,2,1,0:T(8,128)(2,1)S(1)} fusion(s32[]{:T(128)S(6)} %select_n.13, f32[8,4,64,128]{3,2,1,0:T(8,128)} %density.3, f32[1,4,64,128]{3,2,1,0:T(8,128)} %bitcast.4), kind=kLoop, calls=%fused_computation.3 | loop fusion | flops 147456 | bytes 1474564 | tf_op jit(solution)/shard_map/convert_element_type | solution.py:357
  1.2 1.9 %collective-permute-start.1 = (bf16[18,64,128]{2,1,0:T(8,128)(2,1)S(1)}, bf16[18,64,128]{2,1,0:T(8,128)(2,1)S(1)}, u32[]{:S(2)}, u32[]{:S(2)}) collective-permute-start(bf16[18,64,128]{2,1,0:T(8,128)(2,1)S(1)} %bitcast.7), channel_id=1, source_target_pairs={{1,2},{2,1},{3,4},{4,3},{5,6},{6,5},{7,8},{8,7},{9,10},{10,9},{11,... | collective-permute-start | bytes 884744 | tf_op jit(solution)/shard_map/ppermute | solution.py:358
  3.2 0.0 copy-done.1
  3.2 0.0 copy-done
  3.2 0.2 shard_map.73
  3.4 5.3 %collective-permute-start = (bf16[68,16,128]{2,1,0:T(8,128)(2,1)S(1)}, bf16[68,16,128]{2,1,0:T(8,128)(2,1)S(1)}, u32[]{:S(2)}, u32[]{:S(2)}) collective-permute-start(bf16[68,16,128]{2,1,0:T(8,128)(2,1)S(1)} %get-tuple-element.16), channel_id=1, source_target_pairs={{0,1},{1,0},{2,3},{3,2},{4,5},{5,4},{6,7},{7,6},{8,9},{9,8},{10,11... | collective-permute-start | bytes 835592 | tf_op jit(solution)/shard_map/ppermute | solution.py:369
  8.7 0.0 copy-done.2
  8.7 0.0 copy-done.3
  8.7 0.0 copy-done.4
  8.7 0.0 copy-done.5
  8.7 0.0 copy-done.6
  8.7 2.1 %shard_map.74 = (f32[4,66,8,128]{3,2,1,0:T(8,128)S(1)}, f32[4,64,8,128]{3,2,1,0:T(8,128)S(1)}, f32[4,64,8,128]{3,2,1,0:T(8,128)S(1)}, f32[4,8,128]{2,1,0:T(8,128)S(1)}, bf16[128,2432]{1,0:T(8,128)(2,1)S(1)}) custom-call(f32[1,8]{1,0:T(1,128)S(1)} %bitcast.5, f32[1,8]{1,0:T(1,128)S(1)} %bitcast.6, f32[8,4,64,128]{3,2,1,0:T(8,128)S(1)} %copy-done, ...), custom_call_target="tpu_custom_call" | custom-call | tf_op jit(solution)/shard_map/pallas_call | solution.py:370
  10.8 0.0 collective-permute-done.message
  10.8 0.5 shard_map.75
  11.2 1.2 %collective-permute-done.1.message = bf16[18,64,128]{2,1,0:T(8,128)(2,1)S(1)} collective-permute-done((bf16[18,64,128]{2,1,0:T(8,128)(2,1)S(1)}, bf16[18,64,128]{2,1,0:T(8,128)(2,1)S(1)}, u32[]{:S(2)}, u32[]{:S(2)}) %collective-permute-start.1) | collective-permute-done | bytes 294944 | tf_op jit(solution)/shard_map/ppermute | solution.py:358
  12.4 0.5 shard_map.76
  13.0 23.3 %all_to_all.10.cells = bf16[8,16,16,128]{3,2,1,0:T(8,128)(2,1)S(1)} all-to-all(bf16[8,16,16,128]{3,2,1,0:T(8,128)(2,1)S(1)} %get-tuple-element.25), channel_id=1, replica_groups=mesh['sec'=8,'space'=64] {'sec'}, dimensions={0} | all-to-all | bytes 1048576 | tf_op jit(solution)/shard_map/all_to_all | solution.py:399
  36.3 3.2 %shard_map.77 = bf16[8,16,16,128]{3,2,1,0:T(8,128)(2,1)S(1)} custom-call(bf16[8,16,16,128]{3,2,1,0:T(8,128)(2,1)S(1)} %all_to_all.10.cells, bf16[128,2432]{1,0:T(8,128)(2,1)S(1)} %get-tuple-element.26.table), custom_call_target="tpu_custom_call" | custom-call | tf_op jit(solution)/shard_map/pallas_call | solution.py:401
  39.5 21.3 %all_to_all.11.tendency = bf16[8,16,16,128]{3,2,1,0:T(8,128)(2,1)S(1)} all-to-all(bf16[8,16,16,128]{3,2,1,0:T(8,128)(2,1)S(1)} %shard_map.77), channel_id=1, replica_groups=mesh['sec'=8,'space'=64] {'sec'}, dimensions={0} | all-to-all | bytes 1048576 | tf_op jit(solution)/shard_map/all_to_all | solution.py:406
  60.8 1.1 %shard_map.78 = f32[8,4,64,128]{3,2,1,0:T(8,128)} custom-call(f32[2,64,8,128]{3,2,1,0:T(8,128)S(1)} %get-tuple-element.22.near, f32[2,64,8,128]{3,2,1,0:T(8,128)S(1)} %get-tuple-element.24.far, bf16[8,16,16,128]{3,2,1,0:T(8,128)(2,1)S(1)} %all_to_all.11.tendency), custom_call_target="tpu_custom_call" | custom-call | tf_op jit(solution)/shard_map/pallas_call | solution.py:407
  (4 shorter events, 0.0 us)
Async XLA Ops:
  0.0 3.2 %copy-start = (f32[8,4,64,128]{3,2,1,0:T(8,128)S(1)}, f32[8,4,64,128]{3,2,1,0:T(8,128)}, u32[]{:S(2)}) copy-start(f32[8,4,64,128]{3,2,1,0:T(8,128)} %density.3) | copy-start | bytes 3145732
  0.0 3.2 %copy-start.1 = (f32[4,64,128]{2,1,0:T(8,128)S(1)}, f32[4,64,128]{2,1,0:T(8,128)}, u32[]{:S(2)}) copy-start(f32[4,64,128]{2,1,0:T(8,128)} %wind.5) | copy-start | bytes 393220
  0.0 8.7 %copy-start.2 = (f32[64,64]{1,0:T(8,128)S(1)}, f32[64,64]{1,0:T(8,128)}, u32[]{:S(2)}) copy-start(f32[64,64]{1,0:T(8,128)} %kernel.1) | copy-start | bytes 49156
  0.0 8.7 %copy-start.3 = (s32[64,64]{1,0:T(8,128)S(1)}, s32[64,64]{1,0:T(8,128)}, u32[]{:S(2)}) copy-start(s32[64,64]{1,0:T(8,128)} %target.1) | copy-start | bytes 49156
  0.0 8.7 %copy-start.4 = (bf16[64,64]{1,0:T(8,128)(2,1)S(1)}, bf16[64,64]{1,0:T(8,128)(2,1)}, u32[]{:S(2)}) copy-start(bf16[64,64]{1,0:T(8,128)(2,1)} %breakup.1) | copy-start | bytes 24580
  0.0 8.7 %copy-start.5 = (f32[8]{0:T(128)S(1)}, f32[8]{0:T(128)}, u32[]{:S(2)}) copy-start(f32[8]{0:T(128)} %param.9) | copy-start | bytes 100
  0.0 8.7 %copy-start.6 = (f32[8]{0:T(128)S(1)}, f32[8]{0:T(128)}, u32[]{:S(2)}) copy-start(f32[8]{0:T(128)} %param.10) | copy-start | bytes 100
  1.2 11.2 %collective-permute-start.1 = (bf16[18,64,128]{2,1,0:T(8,128)(2,1)S(1)}, bf16[18,64,128]{2,1,0:T(8,128)(2,1)S(1)}, u32[]{:S(2)}, u32[]{:S(2)}) collective-permute-start(bf16[18,64,128]{2,1,0:T(8,128)(2,1)S(1)} %bitcast.7), channel_id=1, source_target_pairs={{1,2},{2,1},{3,4},{4,3},{5,6},{6,5},{7,8},{8,7},{9,10},{10,9},{11,... | collective-permute-start | bytes 884744 | tf_op jit(solution)/shard_map/ppermute | solution.py:358
  3.4 7.4 %collective-permute-start = (bf16[68,16,128]{2,1,0:T(8,128)(2,1)S(1)}, bf16[68,16,128]{2,1,0:T(8,128)(2,1)S(1)}, u32[]{:S(2)}, u32[]{:S(2)}) collective-permute-start(bf16[68,16,128]{2,1,0:T(8,128)(2,1)S(1)} %get-tuple-element.16), channel_id=1, source_target_pairs={{0,1},{1,0},{2,3},{3,2},{4,5},{5,4},{6,7},{7,6},{8,9},{9,8},{10,11... | collective-permute-start | bytes 835592 | tf_op jit(solution)/shard_map/ppermute | solution.py:369

commit v5 on v4

--- a/solution.py
+++ b/solution.py
@@ -18,7 +18,7 @@
 PAIRS = HALF // 2
 STEP = 0.25
 BLOCKS = 36
-DEPTH = BLOCKS * S + 2 * S
+DEPTH = BLOCKS * S + S
 LIMIT = 48 * 1024 * 1024
 
 
@@ -119,9 +119,8 @@
         one = jnp.where(to == k, rate, 0.0) + jnp.where(to_t == k, rate_t, 0.0)
         table[0:S, t * NZ : (t + 1) * NZ] = one.astype(BF)
     table[S:, : BLOCKS * S] = jnp.zeros((S, BLOCKS * S), BF)
-    none = jnp.zeros((S, S), F32)
-    table[0:S, BLOCKS * S :] = jnp.concatenate([breakup[...].astype(F32), none], 1).astype(BF)
-    table[S:, BLOCKS * S :] = jnp.concatenate([rates, none], 1).astype(BF)
+    table[0:S, BLOCKS * S :] = breakup[...]
+    table[S:, BLOCKS * S :] = rates.astype(BF)
 
 
 def spread_rows(rows):
@@ -293,8 +292,6 @@
 
 
 def kinetics_body(cells, table, out, wide, products):
-    products[DEPTH - S :, :] = jnp.zeros((S, 2 * NZ * WIDE), BF)
-
     def step(q, _):
         parts = []
         for u in range(WIDE):
@@ -312,7 +309,7 @@
                 else:
                     rows.append(n[8 * t : 8 * t + 8] * n_i)
             products[S * b : S * (b + 1), :] = jnp.concatenate(rows, 0).astype(BF)
-        products[BLOCKS * S : BLOCKS * S + S, :] = n.astype(BF)
+        products[BLOCKS * S :, :] = n.astype(BF)
         sums = jnp.dot(table[...], products[...], preferred_element_type=F32)
         total = sums[0:S] - n * sums[S:]
         for u in range(WIDE):
@@ -355,8 +352,12 @@
 
     both = jnp.concatenate([density, wind_speed[None]], 0)
     to_other = lax.dynamic_slice_in_dim(both, 2 * odd, 2, 1).astype(BF).reshape(2 * OWN + 2, NY, NZ)
+    to_other, density, wind_held, settling, diffusion, breakup, coag_kernel, pair_target = (
+        lax.optimization_barrier(
+            (to_other, density, wind_speed, settling, diffusion, breakup, coag_kernel, pair_target)
+        )
+    )
     other = lax.ppermute(to_other, "space", [(i, ((i + 1) ^ 1) - 1) for i in range(1, slabs - 1)])
-    wind_held = lax.optimization_barrier(wind_speed)
     to_partner, kept = call(
         pack_body,
         (message, jax.ShapeDtypeStruct((2, NY + 2, OWN, NZ), F32)),
@@ -378,14 +379,14 @@
         ),
         scratch=(pltpu.VMEM(padded, F32), pltpu.VMEM((4, BLOCKS, NZ), F32)),
     )(
-        settling.reshape(1, OWN), diffusion.reshape(1, OWN), density, kept, wind_speed,
+        settling.reshape(1, OWN), diffusion.reshape(1, OWN), density, kept, wind_held,
         coag_kernel, pair_target, breakup,
     )
     half = jax.ShapeDtypeStruct((2, NY, OWN, NZ), F32)
     half_block = jax.ShapeDtypeStruct((4, PAIRS, 16, NZ), BF)
     row_block = (NY + 2, OWN, NZ)
     scratch = (pltpu.VMEM(row_block, F32), pltpu.VMEM(row_block, F32), pltpu.VMEM((NY, OWN, NZ), F32))
-    rest = (wind_speed, old, inner, reach, constants)
+    rest = (wind_held, old, inner, reach, constants)
     near, near_rounded = call(
         functools.partial(side_body, False, slabs),
         (half, half_block),

time: 62.1 us -> 62.1 us (level)
  no operation moved by 1% of the time
where the time goes in v5:
time: 62.1 us; the launch traced here: 61.9 us
  blocking collectives  44.6 us (72%)
  Pallas kernels  7.48 us (12%)
  starting transfers between devices  7.17 us (12%)
  waiting for transfers between devices  1.23 us (2%)
  other arithmetic  1.19 us (2%)
    all_to_all x1, blocking collectives, per_device(): lax.all_to_all(rounded, 'sec', split_axis=0, concat_axis=0, tiled=True)  23.3 us
    all_to_all x1, blocking collectives, per_device(): lax.all_to_all(tendency, 'sec', split_axis=0, concat_axis=0, tiled=True)  21.3 us
    ppermute x1, starting transfers between devices, per_device(): lax.ppermute(to_partner, 'space', [(i, i ^ 1) for i in range(slabs)])  5.25 us
    pallas_call x1, Pallas kernels, per_device(): call(kinetics_body, block, scratch=(pltpu.VMEM((S, width), F32), pltpu.VM...  3.23 us
    pallas_call x1, Pallas kernels, per_device(): call(inner_body, (jax.ShapeDtypeStruct(padded, F32), cells_f32, cells_f32...  2.02 us
    ppermute x1, starting transfers between devices, per_device(): lax.ppermute(to_other, 'space', [(i, (i + 1 ^ 1) - 1) for i in range(1, s...  1.92 us
  transfers between devices with their start and end apart: 2, of which 1 were waited for; matrix products, arithmetic and copies ran while one was open for 0% of the time, Pallas kernels for 4%

profile of v5, /device:TPU:216, one launch (start us, length us, event | category | flops | bytes accessed | tf_op | source)
XLA Modules:
  0.0 61.9 jit_solution(17646888893240228980)
XLA Ops:
  0.0 0.0 copy-start.3
  0.0 0.0 copy-start.4
  0.0 0.0 copy-start.5
  0.0 0.0 copy-start.6
  0.0 1.2 %fusion.1 = bf16[9,2,64,128]{3,2,1,0:T(8,128)(2,1)S(1)} fusion(s32[]{:T(128)S(6)} %select_n.11, f32[8,4,64,128]{3,2,1,0:T(8,128)} %density.1, f32[1,4,64,128]{3,2,1,0:T(8,128)} %bitcast.4), kind=kLoop, calls=%fused_computation.3 | loop fusion | flops 147456 | bytes 1474564 | tf_op jit(solution)/shard_map/convert_element_type | solution.py:354
  1.2 1.9 %collective-permute-start.1 = (bf16[18,64,128]{2,1,0:T(8,128)(2,1)S(1)}, bf16[18,64,128]{2,1,0:T(8,128)(2,1)S(1)}, u32[]{:S(2)}, u32[]{:S(2)}) collective-permute-start(bf16[18,64,128]{2,1,0:T(8,128)(2,1)S(1)} %bitcast.7), channel_id=1, source_target_pairs={{1,2},{2,1},{3,4},{4,3},{5,6},{6,5},{7,8},{8,7},{9,10},{10,9},{11,... | collective-permute-start | bytes 884744 | tf_op jit(solution)/shard_map/ppermute | solution.py:360
  3.2 0.0 copy-done.1
  3.2 0.0 copy-done
  3.2 0.2 shard_map.73
  3.4 5.3 %collective-permute-start = (bf16[68,16,128]{2,1,0:T(8,128)(2,1)S(1)}, bf16[68,16,128]{2,1,0:T(8,128)(2,1)S(1)}, u32[]{:S(2)}, u32[]{:S(2)}) collective-permute-start(bf16[68,16,128]{2,1,0:T(8,128)(2,1)S(1)} %get-tuple-element.26), channel_id=1, source_target_pairs={{0,1},{1,0},{2,3},{3,2},{4,5},{5,4},{6,7},{7,6},{8,9},{9,8},{10,11... | collective-permute-start | bytes 835592 | tf_op jit(solution)/shard_map/ppermute | solution.py:370
  8.7 0.0 copy-done.2
  8.7 0.0 copy-done.3
  8.7 0.0 copy-done.4
  8.7 0.0 copy-done.5
  8.7 0.0 copy-done.6
  8.7 2.0 %shard_map.74 = (f32[4,66,8,128]{3,2,1,0:T(8,128)S(1)}, f32[4,64,8,128]{3,2,1,0:T(8,128)S(1)}, f32[4,64,8,128]{3,2,1,0:T(8,128)S(1)}, f32[4,8,128]{2,1,0:T(8,128)S(1)}, bf16[128,2368]{1,0:T(8,128)(2,1)S(1)}) custom-call(f32[1,8]{1,0:T(1,128)S(1)} %bitcast.5, f32[1,8]{1,0:T(1,128)S(1)} %bitcast.6, f32[8,4,64,128]{3,2,1,0:T(8,128)S(1)} %copy-done, ...), custom_call_target="tpu_custom_call" | custom-call | tf_op jit(solution)/shard_map/pallas_call | solution.py:371
  10.7 0.0 collective-permute-done.message
  10.8 0.5 shard_map.75
  11.2 1.2 %collective-permute-done.1.message = bf16[18,64,128]{2,1,0:T(8,128)(2,1)S(1)} collective-permute-done((bf16[18,64,128]{2,1,0:T(8,128)(2,1)S(1)}, bf16[18,64,128]{2,1,0:T(8,128)(2,1)S(1)}, u32[]{:S(2)}, u32[]{:S(2)}) %collective-permute-start.1) | collective-permute-done | bytes 294944 | tf_op jit(solution)/shard_map/ppermute | solution.py:360
  12.4 0.5 shard_map.76
  13.0 23.3 %all_to_all.10.cells = bf16[8,16,16,128]{3,2,1,0:T(8,128)(2,1)S(1)} all-to-all(bf16[8,16,16,128]{3,2,1,0:T(8,128)(2,1)S(1)} %get-tuple-element.41), channel_id=1, replica_groups=mesh['sec'=8,'space'=64] {'sec'}, dimensions={0} | all-to-all | bytes 1048576 | tf_op jit(solution)/shard_map/all_to_all | solution.py:400
  36.3 3.2 %shard_map.77 = bf16[8,16,16,128]{3,2,1,0:T(8,128)(2,1)S(1)} custom-call(bf16[8,16,16,128]{3,2,1,0:T(8,128)(2,1)S(1)} %all_to_all.10.cells, bf16[128,2368]{1,0:T(8,128)(2,1)S(1)} %get-tuple-element.42.table), custom_call_target="tpu_custom_call" | custom-call | tf_op jit(solution)/shard_map/pallas_call | solution.py:402
  39.5 21.3 %all_to_all.11.tendency = bf16[8,16,16,128]{3,2,1,0:T(8,128)(2,1)S(1)} all-to-all(bf16[8,16,16,128]{3,2,1,0:T(8,128)(2,1)S(1)} %shard_map.77), channel_id=1, replica_groups=mesh['sec'=8,'space'=64] {'sec'}, dimensions={0} | all-to-all | bytes 1048576 | tf_op jit(solution)/shard_map/all_to_all | solution.py:407
  60.8 1.1 %shard_map.78 = f32[8,4,64,128]{3,2,1,0:T(8,128)} custom-call(f32[2,64,8,128]{3,2,1,0:T(8,128)S(1)} %get-tuple-element.37.near, f32[2,64,8,128]{3,2,1,0:T(8,128)S(1)} %get-tuple-element.40.far, bf16[8,16,16,128]{3,2,1,0:T(8,128)(2,1)S(1)} %all_to_all.11.tendency), custom_call_target="tpu_custom_call" | custom-call | tf_op jit(solution)/shard_map/pallas_call | solution.py:408
  (4 shorter events, 0.0 us)
Async XLA Ops:
  0.0 3.2 %copy-start = (f32[8,4,64,128]{3,2,1,0:T(8,128)S(1)}, f32[8,4,64,128]{3,2,1,0:T(8,128)}, u32[]{:S(2)}) copy-start(f32[8,4,64,128]{3,2,1,0:T(8,128)} %density.1) | copy-start | bytes 3145732
  0.0 3.2 %copy-start.1 = (f32[4,64,128]{2,1,0:T(8,128)S(1)}, f32[4,64,128]{2,1,0:T(8,128)}, u32[]{:S(2)}) copy-start(f32[4,64,128]{2,1,0:T(8,128)} %wind.2) | copy-start | bytes 393220
  0.0 8.7 %copy-start.2 = (f32[64,64]{1,0:T(8,128)S(1)}, f32[64,64]{1,0:T(8,128)}, u32[]{:S(2)}) copy-start(f32[64,64]{1,0:T(8,128)} %kernel) | copy-start | bytes 49156
  0.0 8.7 %copy-start.3 = (s32[64,64]{1,0:T(8,128)S(1)}, s32[64,64]{1,0:T(8,128)}, u32[]{:S(2)}) copy-start(s32[64,64]{1,0:T(8,128)} %target) | copy-start | bytes 49156
  0.0 8.7 %copy-start.4 = (bf16[64,64]{1,0:T(8,128)(2,1)S(1)}, bf16[64,64]{1,0:T(8,128)(2,1)}, u32[]{:S(2)}) copy-start(bf16[64,64]{1,0:T(8,128)(2,1)} %breakup) | copy-start | bytes 24580
  0.0 8.7 %copy-start.5 = (f32[8]{0:T(128)S(1)}, f32[8]{0:T(128)}, u32[]{:S(2)}) copy-start(f32[8]{0:T(128)} %param.9) | copy-start | bytes 100
  0.0 8.7 %copy-start.6 = (f32[8]{0:T(128)S(1)}, f32[8]{0:T(128)}, u32[]{:S(2)}) copy-start(f32[8]{0:T(128)} %param.10) | copy-start | bytes 100
  1.2 11.2 %collective-permute-start.1 = (bf16[18,64,128]{2,1,0:T(8,128)(2,1)S(1)}, bf16[18,64,128]{2,1,0:T(8,128)(2,1)S(1)}, u32[]{:S(2)}, u32[]{:S(2)}) collective-permute-start(bf16[18,64,128]{2,1,0:T(8,128)(2,1)S(1)} %bitcast.7), channel_id=1, source_target_pairs={{1,2},{2,1},{3,4},{4,3},{5,6},{6,5},{7,8},{8,7},{9,10},{10,9},{11,... | collective-permute-start | bytes 884744 | tf_op jit(solution)/shard_map/ppermute | solution.py:360
  3.4 7.3 %collective-permute-start = (bf16[68,16,128]{2,1,0:T(8,128)(2,1)S(1)}, bf16[68,16,128]{2,1,0:T(8,128)(2,1)S(1)}, u32[]{:S(2)}, u32[]{:S(2)}) collective-permute-start(bf16[68,16,128]{2,1,0:T(8,128)(2,1)S(1)} %get-tuple-element.26), channel_id=1, source_target_pairs={{0,1},{1,0},{2,3},{3,2},{4,5},{5,4},{6,7},{7,6},{8,9},{9,8},{10,11... | collective-permute-start | bytes 835592 | tf_op jit(solution)/shard_map/ppermute | solution.py:370
